TPU v7x, 256 devices: a whole 4x4x8 slice. The times are simulated.
256 devices in a mesh: col: 32 (over y, z), grp: 8 (over x, core).
Axes of the slice: x: 4, y: 4, z: 8, core: 2. Of those that a mesh axis runs over, the one named last changes fastest.
Arguments:
- velocity_cotangent: float32 [20, 8388608], P(None, ('col', 'grp')), may hold values from -6 to 6
- vertical_inverse: float32 [20, 20], replicated, may hold values from -1.25 to 1.25
- sliding_speed: float32 [8388608], P(('col', 'grp')), may hold values from 0.3 to 3
- friction_coef: float32 [8388608], P(('col', 'grp')), may hold values from 0.3 to 3
- thawed_bed: int32 [8388608], P(('col', 'grp')), may hold values 0 or 1
- basal_melt: float32 [8388608], P(('col', 'grp')), may hold values from 0 to 1
- storage_coef: float32 [8388608], P(('col', 'grp')), may hold values from 0.1 to 3
- owner_tile: int32 [8388608, 1], P(('col', 'grp')), may hold values from 0 to 31, as said below
- channel_open: int32 [256, 40960], P('grp', 'col'), may hold values 0 or 1
- group_mix: float32 [8, 8], replicated, may hold values from -2 to 2
- control_map: bfloat16 [16384, 32768], P(('col', 'grp')), may hold values from -0.03125 to 0.03125
Outputs:
- velocity_adjoint: float32 [20, 8388608], P(None, ('col', 'grp'))
- pressure_adjoint: float32 [256, 40960], P('grp', 'col')
- friction_sensitivity: float32 [8388608], P(('col', 'grp'))
- friction_gradient: float32 [16384], P(('col', 'grp'))
Inputs may be any that keep to these rules, and one draw needn't show every extreme that they name: `owner_tile`: within each device's block of 32768 columns the tile indices never fall, no tile index appears more than 1280 times, and some tile index appears exactly 1280 times.
All inputs are finite; a program needn't handle non-finite values. No bound on the sum of `thawed_bed` or of `channel_open` on one device may be relied on, other than what follows from the above.
Results may differ from a plain program's by a relative error of at most 0.0027.
The roundings to bfloat16 on the way count: a program that leaves them out, or rounds other values in their place, can miss the bound.
Values sent between devices are 32-bit elements; how exact they have to be, the bound alone decides.
A program may use at most 64 MiB of HBM per device.

v0:
```python
import jax
import jax.numpy as jnp
from jax import lax
from jax.sharding import PartitionSpec as P

HSWEEPS = 4


diffusion_rate = 0.12
melt_rate = 0.3


def extended(block, sides, width):
    for axis, dim in sides:
        count = lax.axis_size(axis)
        forward = [(i, i + 1) for i in range(count - 1)]
        backward = [(target, source) for source, target in forward]
        low = lax.ppermute(
            lax.slice_in_dim(block, block.shape[dim] - width, None, axis=dim), axis, forward
        )
        high = lax.ppermute(lax.slice_in_dim(block, 0, width, axis=dim), axis, backward)
        block = jnp.concatenate([low, block, high], axis=dim)
    return block


def stencil_step(field, keep, coef):
    beside_all = field[2:, 1:-1] + field[:-2, 1:-1] + field[1:-1, 2:] + field[1:-1, :-2]
    centre = field[1:-1, 1:-1]
    return keep * centre + coef * (beside_all - 4.0 * centre)


def on_device(
    velocity_cotangent,
    vertical_inverse,
    sliding_speed,
    friction_coef,
    thawed_bed,
    basal_melt,
    storage_coef,
    owner_tile,
    channel_open,
    group_mix,
    control_map,
):
    tiles = lax.axis_size("col")
    columns = sliding_speed.shape[0]
    capacity = 5 * (columns // tiles) // 4
    adjoint = jnp.dot(
        vertical_inverse.T,
        velocity_cotangent,
        precision=lax.Precision.HIGHEST,
        preferred_element_type=jnp.float32,
    )
    thawed = thawed_bed.astype(jnp.float32)
    basal = thawed * sliding_speed * adjoint[adjoint.shape[0] - 1]
    source = friction_coef * basal
    targets = owner_tile[:, 0]
    tile_ids = jnp.arange(tiles, dtype=jnp.int32)
    counts = jnp.sum((targets[:, None] == tile_ids[None, :]).astype(jnp.int32), axis=0)
    starts = jnp.cumsum(counts) - counts
    slot_range = jnp.arange(capacity, dtype=jnp.int32)
    values = jnp.stack([source, basal_melt, storage_coef])
    values_pad = jnp.concatenate([values, jnp.zeros((3, capacity), jnp.float32)], axis=1)

    def place_tile(tile):
        window = lax.dynamic_slice_in_dim(values_pad, starts[tile], capacity, 1)
        return jnp.where(slot_range[None, :] < counts[tile], window, 0.0)

    packed = lax.map(place_tile, tile_ids)
    received = lax.all_to_all(packed, "col", split_axis=0, concat_axis=0, tiled=True)
    conduct = jnp.where(channel_open == 1, 1.0, 0.25).astype(jnp.float32)
    pressure = received[:, 0]
    coef = diffusion_rate * conduct / (1.0 + received[:, 2])
    keep = 1.0 - melt_rate * received[:, 1]
    for sweep in range(HSWEEPS):
        padded = extended(pressure, (("col", 1), ("grp", 0)), 1)
        pressure = stencil_step(padded, keep, coef)
    returned = lax.all_to_all(pressure, "col", split_axis=0, concat_axis=0, tiled=True)

    def add_tile(tile, total):
        row_back = lax.dynamic_index_in_dim(returned, tile, 0, keepdims=False)
        placed = lax.dynamic_update_slice_in_dim(
            jnp.zeros((columns + capacity,), jnp.float32), row_back, starts[tile], 0
        )[:columns]
        return total + jnp.where(targets == tile, placed, 0.0)

    back = lax.fori_loop(0, tiles, add_tile, jnp.zeros((columns,), jnp.float32))
    sensitivity = thawed * friction_coef * (basal + back)
    member = lax.axis_index("grp")
    row_mix = lax.dynamic_index_in_dim(group_mix, member, 0, keepdims=False)
    piece = lax.all_gather(sensitivity, "grp", axis=0, tiled=True)
    count = piece.shape[0] // columns
    mixed = jnp.sum(row_mix[:, None] * piece.reshape(count, columns), axis=0)
    mixed_bf = mixed.astype(jnp.bfloat16)
    gradient = jnp.dot(control_map, mixed_bf, preferred_element_type=jnp.float32)
    return (adjoint, pressure, sensitivity, gradient)


def solution(mesh):
    in_specs = (
        P(None, ("col", "grp")),
        P(),
        P(("col", "grp")),
        P(("col", "grp")),
        P(("col", "grp")),
        P(("col", "grp")),
        P(("col", "grp")),
        P(("col", "grp"), None),
        P("grp", "col"),
        P(),
        P(("col", "grp"), None),
    )
    out_specs = (P(None, ("col", "grp")), P("grp", "col"), P(("col", "grp")), P(("col", "grp")))
    return jax.shard_map(
        on_device, mesh=mesh, in_specs=in_specs, out_specs=out_specs, check_vma=False
    )
```

profile of v0, /device:TPU:1, one launch (start us, length us, event | category | flops | bytes accessed | tf_op | source)
XLA Modules:
  0.0 605.6 jit_solution(172107074482019597)
XLA Ops:
  7.2 2.1 convert_reduce_fusion
  12.8 3.6 fusion.38
  16.4 1.7 copy-done.2
  20.1 267.4 %while.25 = (s32[]{:T(128)}, f32[32,3,1280]{2,1,0:T(4,128)}, s32[32]{0:T(128)S(1)}, s32[32]{0:T(128)S(1)}, s32[32]{0:T(128)}, /*index=5*/f32[3,34048]{1,0:T(4,128)}, s32[]{:T(128)}, s32[]{:T(128)}, s32[]{:T(128)}, s32[]{:T(128)}) while((s32[]{:T(128)}, f32[32,3,1280]{2,1,0:T(4,128)}, s32[32]{0:T(128)S(1)}, s32[32]{0:T(128)S(1)}, ...), condition=%wide.region_3.4_spmd.clone, body=%wide.region_2.3_spmd.clone.sunk | while | flops 5128 | bytes 44245 | solution.py:69
  27.0 1.4 bitcast_dynamic-update-slice_fusion.2
  35.4 1.4 bitcast_dynamic-update-slice_fusion.2
  52.1 1.4 bitcast_dynamic-update-slice_fusion.2
  85.5 1.4 bitcast_dynamic-update-slice_fusion.2
  144.0 1.4 bitcast_dynamic-update-slice_fusion.2
  169.0 1.4 bitcast_dynamic-update-slice_fusion.2
  210.8 1.4 bitcast_dynamic-update-slice_fusion.2
  235.9 1.4 bitcast_dynamic-update-slice_fusion.2
  252.6 1.4 bitcast_dynamic-update-slice_fusion.2
  277.7 1.4 bitcast_dynamic-update-slice_fusion.2
  287.5 28.4 %all_to_all.17 = f32[32,3,1280]{2,1,0:T(4,128)S(1)} all-to-all(f32[32,3,1280]{2,1,0:T(4,128)} %get-tuple-element.135), channel_id=1, replica_groups=mesh['col'=32,'grp'=8] {'col'}, dimensions={0} | all-to-all | bytes 983040 | tf_op jit(solution)/shard_map/all_to_all | solution.py:70
  317.7 5.2 collective-permute-start
  324.2 3.2 collective-permute-done.1
  327.4 1.7 concatenate.68
  329.9 6.4 %collective-permute-start.2 = (f32[1,1282]{1,0:T(1,128)S(1)}, f32[1,1282]{1,0:T(1,128)S(1)}, u32[]{:S(2)}, u32[]{:S(2)}) collective-permute-start(f32[1,1282]{1,0:T(1,128)S(1)} %get-tuple-element.202), channel_id=1, source_target_pairs={{1,0},{2,1},{3,2},{4,3},{5,4},{6,5},{7,6},{9,8},{10,9},{11,10},{12... | collective-permute-start | bytes 15392 | tf_op jit(solution)/shard_map/ppermute | solution.py:21
  336.3 3.0 collective-permute-start.3
  340.1 2.2 fusion.24
  343.0 1.8 collective-permute-start.4
  346.1 3.2 collective-permute-done.5
  349.3 1.7 concatenate.73
  351.8 2.8 collective-permute-start.6
  354.6 4.7 collective-permute-start.7
  360.1 1.6 fusion.18
  362.4 3.3 collective-permute-start.8
  367.1 3.2 collective-permute-done.9
  370.2 1.7 concatenate.78
  372.8 1.9 collective-permute-start.10
  374.7 5.6 collective-permute-start.11
  381.1 1.6 fusion.12
  383.4 2.8 collective-permute-start.12
  387.6 3.2 collective-permute-done.13
  390.7 1.7 concatenate.83
  393.3 1.9 collective-permute-start.14
  395.2 5.6 collective-permute-start.15
  401.6 1.6 fusion.6
  404.7 9.6 %all-to-all-start.1 = ((f32[32,1,1280]{2,1,0:T(1,128)}), f32[32,1,1280]{2,1,0:T(1,128)}, u32[]{:S(2)}, u32[]{:S(2)}) async-start(f32[32,1,1280]{2,1,0:T(1,128)} %copy.28), calls=%async_computation.1 | async-start | bytes 327680 | tf_op jit(solution)/shard_map/all_to_all | solution.py:78
  414.3 9.4 %all-to-all-done.1 = f32[32,1,1280]{2,1,0:T(1,128)} async-done(((f32[32,1,1280]{2,1,0:T(1,128)}), f32[32,1,1280]{2,1,0:T(1,128)}, u32[]{:S(2)}, u32[]{:S(2)}) %all-to-all-start.1) | async-done | bytes 163872 | tf_op jit(solution)/shard_map/all_to_all | solution.py:78
  423.7 1.6 copy.51
  425.3 140.0 %while.26 = (s32[]{:T(128)}, f32[32768]{0:T(1024)S(1)}, s32[32768]{0:T(1024)S(1)}, f32[32,1280]{1,0:T(8,128)}, s32[32]{0:T(128)}, /*index=5*/s32[]{:T(128)}, f32[]{:T(128)}, s32[]{:T(128)}, s32[]{:T(128)}) while((s32[]{:T(128)}, f32[32768]{0:T(1024)S(1)}, s32[32768]{0:T(1024)S(1)}, f32[32,1280]{1,0:T(8,128)}, s32[32]{0:T(128)}, ...), condition=%wide.region_5.6_spmd.clone, body=%wide.region_4.5_spmd.clone.sunk | while | flops 131078 | bytes 681125 | solution.py:87
  565.3 1.8 add_multiply_fusion
  567.8 23.0 %all-gather.2.cloned.1.call-done = f32[262144]{0:T(1024)} async-done(((f32[32768]{0:T(1024)}), f32[262144]{0:T(1024)}) %all-gather.2.cloned.1.call-update) | async-done | bytes 1048592 | tf_op jit(solution)/shard_map/all_gather | solution.py:91
  590.8 2.4 reshape.53
  593.1 1.6 multiply_reduce_fusion
  594.8 3.9 convolution_bitcast_fusion
  (380 shorter events, 230.0 us)
Async XLA Ops:
  7.2 5.6 copy-start
  7.2 11.6 %copy-start.10 = (f32[32768]{0:T(1024)S(1)}, f32[32768]{0:T(1024)}, u32[]{:S(2)}) copy-start(f32[32768]{0:T(1024)} %param.17) | copy-start | bytes 393220
  7.2 11.6 %copy-start.9 = (f32[32768]{0:T(1024)S(1)}, f32[32768]{0:T(1024)}, u32[]{:S(2)}) copy-start(f32[32768]{0:T(1024)} %param.18) | copy-start | bytes 393220
  7.2 11.6 %copy-start.11 = (s32[32768]{0:T(1024)S(1)}, s32[32768]{0:T(1024)}, u32[]{:S(2)}) copy-start(s32[32768]{0:T(1024)} %param.19) | copy-start | bytes 393220
  10.7 9.4 %copy-start.14 = (s32[32]{0:T(128)S(1)}, s32[32]{0:T(128)}, u32[]{:S(2)}) copy-start(s32[32]{0:T(128)} %convert_reduce_fusion) | copy-start | bytes 388
  11.5 7.3 %copy-start.12 = (f32[32768]{0:T(1024)S(1)}, f32[32768]{0:T(1024)}, u32[]{:S(2)}) copy-start(f32[32768]{0:T(1024)} %param.21) | copy-start | bytes 393220
  11.5 7.3 %copy-start.13 = (f32[32768]{0:T(1024)S(1)}, f32[32768]{0:T(1024)}, u32[]{:S(2)}) copy-start(f32[32768]{0:T(1024)} %param.20) | copy-start | bytes 393220
  16.4 1.7 copy-start.2
  18.1 0.7 copy-start.7
  315.9 109.4 %copy-start.1 = (s32[32768,1]{0,1:T(1,128)S(1)}, s32[32768,1]{0,1:T(1,128)}, u32[]{:S(2)}) copy-start(s32[32768,1]{0,1:T(1,128)} %param.22) | copy-start | bytes 393220
  316.9 0.7 copy-start.5
  317.7 6.5 %collective-permute-start = (f32[32,1]{1,0:T(8,128)S(1)}, f32[32,1]{1,0:T(8,128)S(1)}, u32[]{:S(2)}, u32[]{:S(2)}) collective-permute-start(f32[32,1]{1,0:T(8,128)S(1)} %get-tuple-element.211), channel_id=1, source_target_pairs={{0,8},{8,16},{16,24},{24,32},{32,40},{40,48},{48,56},{56,64},{64,7... | collective-permute-start | bytes 392 | tf_op jit(solution)/shard_map/ppermute | solution.py:18
  322.9 4.5 collective-permute-start.1
  329.9 9.4 %collective-permute-start.2 = (f32[1,1282]{1,0:T(1,128)S(1)}, f32[1,1282]{1,0:T(1,128)S(1)}, u32[]{:S(2)}, u32[]{:S(2)}) collective-permute-start(f32[1,1282]{1,0:T(1,128)S(1)} %get-tuple-element.202), channel_id=1, source_target_pairs={{1,0},{2,1},{3,2},{4,3},{5,4},{6,5},{7,6},{9,8},{10,9},{11,10},{12... | collective-permute-start | bytes 15392 | tf_op jit(solution)/shard_map/ppermute | solution.py:21
  336.3 3.8 collective-permute-start.3
  342.3 0.7 copy-start.6
  343.0 3.1 collective-permute-start.4
  344.8 4.5 collective-permute-start.5
  351.8 7.6 %collective-permute-start.6 = (f32[1,1282]{1,0:T(1,128)S(1)}, f32[1,1282]{1,0:T(1,128)S(1)}, u32[]{:S(2)}, u32[]{:S(2)}) collective-permute-start(f32[1,1282]{1,0:T(1,128)S(1)} %get-tuple-element.200), channel_id=1, source_target_pairs={{1,0},{2,1},{3,2},{4,3},{5,4},{6,5},{7,6},{9,8},{10,9},{11,10},{12... | collective-permute-start | bytes 15392 | tf_op jit(solution)/shard_map/ppermute | solution.py:21
  354.6 5.5 collective-permute-start.7
  361.7 0.7 copy-start.4
  362.4 4.6 collective-permute-start.8
  365.8 4.5 collective-permute-start.9
  372.8 7.6 %collective-permute-start.10 = (f32[1,1282]{1,0:T(1,128)S(1)}, f32[1,1282]{1,0:T(1,128)S(1)}, u32[]{:S(2)}, u32[]{:S(2)}) collective-permute-start(f32[1,1282]{1,0:T(1,128)S(1)} %get-tuple-element.198), channel_id=1, source_target_pairs={{1,0},{2,1},{3,2},{4,3},{5,4},{6,5},{7,6},{9,8},{10,9},{11,10},{12... | collective-permute-start | bytes 15392 | tf_op jit(solution)/shard_map/ppermute | solution.py:21
  374.7 6.4 %collective-permute-start.11 = (f32[1,1282]{1,0:T(1,128)S(1)}, f32[1,1282]{1,0:T(1,128)S(1)}, u32[]{:S(2)}, u32[]{:S(2)}) collective-permute-start(f32[1,1282]{1,0:T(1,128)S(1)} %get-tuple-element.199), channel_id=1, source_target_pairs={{0,1},{1,2},{2,3},{3,4},{4,5},{5,6},{6,7},{8,9},{9,10},{10,11},{11... | collective-permute-start | bytes 15392 | tf_op jit(solution)/shard_map/ppermute | solution.py:18
  382.7 0.7 copy-start.3
  383.4 4.2 collective-permute-start.12
  386.3 4.5 collective-permute-start.13
  393.3 7.6 %collective-permute-start.14 = (f32[1,1282]{1,0:T(1,128)S(1)}, f32[1,1282]{1,0:T(1,128)S(1)}, u32[]{:S(2)}, u32[]{:S(2)}) collective-permute-start(f32[1,1282]{1,0:T(1,128)S(1)} %get-tuple-element.196), channel_id=1, source_target_pairs={{1,0},{2,1},{3,2},{4,3},{5,4},{6,5},{7,6},{9,8},{10,9},{11,10},{12... | collective-permute-start | bytes 15392 | tf_op jit(solution)/shard_map/ppermute | solution.py:21
  395.2 6.4 %collective-permute-start.15 = (f32[1,1282]{1,0:T(1,128)S(1)}, f32[1,1282]{1,0:T(1,128)S(1)}, u32[]{:S(2)}, u32[]{:S(2)}) collective-permute-start(f32[1,1282]{1,0:T(1,128)S(1)} %get-tuple-element.197), channel_id=1, source_target_pairs={{0,1},{1,2},{2,3},{3,4},{4,5},{5,6},{6,7},{8,9},{9,10},{10,11},{11... | collective-permute-start | bytes 15392 | tf_op jit(solution)/shard_map/ppermute | solution.py:18
  403.2 0.7 copy-start.8
  404.7 19.1 %all-to-all-start.1 = ((f32[32,1,1280]{2,1,0:T(1,128)}), f32[32,1,1280]{2,1,0:T(1,128)}, u32[]{:S(2)}, u32[]{:S(2)}) async-start(f32[32,1,1280]{2,1,0:T(1,128)} %copy.28), calls=%async_computation.1 | async-start | bytes 327680 | tf_op jit(solution)/shard_map/all_to_all | solution.py:78
  414.3 176.5 %all-gather.2.cloned.1.call-start = ((), (), s32[]{:S(2)}) async-start(), calls=%async_computation.2 | async-start | bytes 1179648 | tf_op jit(solution)/shard_map/all_gather | solution.py:91
Sparse Core Ops, SparseCore 0:
  567.2 23.4 all-gather.1
where the time goes:
time: 614 us; the launch traced here: 606 us
  loops' own time  186 us (30%)
  local copies, waits for them, and re-layouts  175 us (29%)
  other arithmetic  85.7 us (14%)
  starting transfers between devices  59.9 us (10%)
  waiting for transfers between devices  48 us (8%)
  blocking collectives  28.4 us (5%)
  between operations  14.4 us (2%)
  matrix products  7.45 us (1%)
    another operation x1, loops' own time, on_device(): packed = lax.map(place_tile, tile_ids)  125 us
    another operation x1, loops' own time, on_device(): back = lax.fori_loop(0, tiles, add_tile, jnp.zeros((columns,), jnp.float32))  61.6 us
    dynamic_update_slice x32, other arithmetic, on_device(): packed = lax.map(place_tile, tile_ids)  45.6 us
    dynamic_slice x32, local copies, waits for them, and re-layouts, add_tile(): starts[tile]  39.9 us
    dynamic_slice x32, local copies, waits for them, and re-layouts, place_tile(): window = lax.dynamic_slice_in_dim(values_pad, starts[tile], capacity, 1)  38.8 us
    ppermute x8, starting transfers between devices, extended(): lax.ppermute(lax.slice_in_dim(block, block.shape[dim] - width, None, axis...  32.1 us
    all_to_all x1, blocking collectives, on_device(): lax.all_to_all(packed, 'col', split_axis=0, concat_axis=0, tiled=True)  28.4 us
    dynamic_slice x32, local copies, waits for them, and re-layouts, add_tile(): row_back = lax.dynamic_index_in_dim(returned, tile, 0, keepdims=False)  25.8 us
  transfers between devices with their start and end apart: 18, of which 10 were waited for; matrix products, arithmetic and copies ran while one was open for 0% of the time, Pallas kernels for 0%

commit v1 on v0

v1 whole, which is shorter than its diff:
```python
import jax
import jax.numpy as jnp
from jax import lax
from jax.experimental import pallas as pl
from jax.experimental.pallas import tpu as pltpu
from jax.sharding import PartitionSpec as P

HSWEEPS = 4
diffusion_rate = 0.12
melt_rate = 0.3

TILES = 32
GROUP = 8
CHIPS = 4
COLUMNS = 32768
LAYERS = 20
LANES = 128
ROWS = COLUMNS // LANES
RUN = 10
MSG = 16
EDGE = 8
WIDE = RUN * LANES + LANES
TALL = TILES + 2 * EDGE
CONTROLS = 64
PARTS = 4
PART = ROWS // PARTS
MESH = pl.DeviceIdType.MESH

LEVELS = ((32, 16, 24), (16, 24, 40), (8, 48, 80), (4, 88, 160), (2, 168, 256))


def rows_at(start, count):
    return pl.ds(pl.multiple_of(start, 8), count)


def kernel(
    mix_ref, inverse_ref, cot_hbm, slide_hbm, fric_hbm, thaw_hbm, melt_hbm, store_hbm, owner_hbm, open_hbm, map_hbm,
    press_hbm, sens_hbm, grad_ref,
    cot, cmap, slide, fric, thaw, melt, store, owner, chan, source, basal,
    send1, send2, recv1, recv2, cond, cond_low, cond_high, coef, pressure, press_out, back_send,
    lev0, lev1, lev2, lev3, lev4, sens, gathered, other_send, other_recv, mine,
    load_sem, cot_sem, self_sem, send_sem, recv_sem, part_send, part_recv, pair_send, pair_recv, out_sem,
):
    a = lax.axis_index("col")
    g = lax.axis_index("grp")
    chip = g // 2
    core = lax.rem(g, 2)
    sibling = chip * 2 + (1 - core)
    up = lax.rem(g + GROUP - 1, GROUP)
    down = lax.rem(g + 1, GROUP)
    left = lax.rem(a + TILES - 1, TILES)
    right = lax.rem(a + 1, TILES)

    def load(src, dst, number):
        copy = pltpu.make_async_copy(src, dst, load_sem.at[number])
        copy.start()
        return copy

    owner_load = load(owner_hbm, owner, 0)
    melt_load = load(melt_hbm, melt.at[pl.ds(0, ROWS)], 1)
    store_load = load(store_hbm, store.at[pl.ds(0, ROWS)], 2)
    chan_load = load(open_hbm, chan, 3)
    cot_loads = []
    piece = COLUMNS // PARTS
    for q in range(PARTS):
        copy = pltpu.make_async_copy(
            cot_hbm.at[:, pl.ds(q * piece, piece)], cot.at[:, pl.ds(q * piece, piece)], cot_sem.at[q]
        )
        copy.start()
        cot_loads.append(copy)
    thaw_load = load(thaw_hbm, thaw, 4)
    slide_load = load(slide_hbm, slide, 5)
    fric_load = load(fric_hbm, fric, 6)
    map_load = load(map_hbm, cmap, 7)

    barrier = pltpu.get_barrier_semaphore()

    def greet(d, carry):
        pl.semaphore_signal(
            barrier, inc=1, device_id={"col": lax.rem(a + d, TILES)}, device_id_type=MESH
        )
        return carry

    lax.fori_loop(1, TILES, greet, 0)
    for other in (up, down):
        pl.semaphore_signal(barrier, inc=1, device_id={"grp": other}, device_id_type=MESH)
    for d in range(1, CHIPS):
        same_core = lax.rem(chip + d, CHIPS) * 2 + core
        pl.semaphore_signal(barrier, inc=1, device_id={"grp": same_core}, device_id_type=MESH)

    lane = lax.broadcasted_iota(jnp.int32, (1, LANES), 1)
    edge_rows = jnp.zeros((4 * MSG, LANES), jnp.float32)
    for ref in (recv1, recv2):
        ref[0 : 4 * MSG, :] = edge_rows
        ref[(TALL - 4) * MSG : TALL * MSG, :] = edge_rows

    owner_load.wait()
    owners = owner[...]
    starts = [jnp.int32(0)]
    for t in range(1, TILES):
        below = jnp.where(owners < t, 1.0, 0.0).astype(jnp.float32)
        partial = jnp.sum(below.reshape(ROWS // 8, 8, LANES), axis=0)
        starts.append(jnp.clip(jnp.sum(partial).astype(jnp.int32), 0, COLUMNS))
    starts.append(jnp.int32(COLUMNS))

    slot = lax.broadcasted_iota(jnp.int32, (MSG, LANES), 0) * LANES + lax.broadcasted_iota(
        jnp.int32, (MSG, LANES), 1
    )

    def window(ref, t):
        first = lax.shift_right_logical(starts[t], 7)
        turn = lax.bitwise_and(starts[t], LANES - 1)
        back_turn = lax.bitwise_and(LANES - turn, LANES - 1)
        low = pltpu.roll(ref[pl.ds(first, MSG), :], back_turn, 1)
        high = pltpu.roll(ref[pl.ds(first + 1, MSG), :], back_turn, 1)
        both = jnp.where(lane < LANES - turn, low, high)
        return jnp.where(slot < starts[t + 1] - starts[t], both, 0.0)

    store_load.wait()
    melt_load.wait()
    for t in range(TILES):
        stored = window(store, t)
        melted = window(melt, t)
        send1[MSG * t : MSG * t + RUN, :] = stored[:RUN]
        send1[MSG * t + RUN : MSG * (t + 1), :] = melted[: MSG - RUN]
        send2[MSG * t : MSG * t + 2 * RUN - MSG, :] = melted[MSG - RUN : RUN]

    chan_load.wait()
    cond[EDGE : EDGE + TILES, : RUN * LANES] = jnp.where(chan[...] == 1, diffusion_rate, 0.25 * diffusion_rate)

    pl.semaphore_wait(barrier, TILES - 1 + 2 + CHIPS - 1)

    def post(src, dst, number, where):
        copy = pltpu.make_async_remote_copy(
            src_ref=src, dst_ref=dst, send_sem=send_sem.at[number], recv_sem=recv_sem.at[number],
            device_id=where, device_id_type=MESH,
        )
        copy.start()
        return copy

    def to_all(src, dst, number, self_number):
        def one(d, carry):
            target = lax.rem(a + d, TILES)
            post(src.at[rows_at(target * MSG, MSG)], dst.at[rows_at((EDGE + a) * MSG, MSG)], number, {"col": target})
            return carry

        lax.fori_loop(1, TILES, one, 0)
        own = pltpu.make_async_copy(
            src.at[rows_at(a * MSG, MSG)], dst.at[rows_at((EDGE + a) * MSG, MSG)], self_sem.at[self_number]
        )
        own.start()
        return own

    def all_done(buffer, rows, sem):
        pltpu.make_async_copy(buffer.at[pl.ds(0, rows)], buffer.at[pl.ds(0, rows)], sem).wait()

    chan_low = post(cond.at[EDGE : EDGE + TILES, (RUN - 1) * LANES : RUN * LANES], cond_low, 0, {"col": right})
    chan_high = post(cond.at[EDGE : EDGE + TILES, 0:LANES], cond_high, 1, {"col": left})
    own1 = to_all(send1, recv1, 2, 0)

    weight = jnp.broadcast_to(inverse_ref[:, LAYERS - 1 : LAYERS], (LAYERS, LANES))
    sublane = lax.broadcasted_iota(jnp.int32, (8, LANES), 0)
    thaw_load.wait()
    slide_load.wait()
    fric_load.wait()
    for q in range(PARTS):
        cot_loads[q].wait()

        def last_layer(j, carry):
            block = jnp.zeros((8, LANES), jnp.float32)
            for k in range(8):
                layers = cot[:, pl.ds(pl.multiple_of(j * 1024 + k * LANES, LANES), LANES)]
                total = jnp.sum(layers * weight, axis=0, keepdims=True)
                block = jnp.where(sublane == k, total, block)
            at = rows_at(j * 8, 8)
            base = thaw[at, :].astype(jnp.float32) * slide[at, :] * block
            basal[at, :] = base
            source[at, :] = fric[at, :] * base
            return carry

        lax.fori_loop(q * 8, (q + 1) * 8, last_layer, 0)

    for t in range(TILES):
        send2[MSG * t + 2 * RUN - MSG : MSG * t + 3 * RUN - MSG, :] = window(source, t)[:RUN]

    tile = lax.broadcasted_iota(jnp.int32, (TILES, LANES), 0)
    lanes = lax.broadcasted_iota(jnp.int32, (TILES, LANES), 1)

    def beside(first, last):
        ahead = jnp.where(tile == TILES - 1, 0.0, pltpu.roll(first, TILES - 1, 0))
        behind = jnp.where(tile == 0, 0.0, pltpu.roll(last, 1, 0))
        return jnp.where(lanes < 4, ahead, jnp.where(lanes >= LANES - 4, behind, 0.0))

    def every(ref, row):
        return ref[pl.ds(row, TILES, stride=MSG), :]

    send2[pl.ds(14, TILES, stride=MSG), :] = beside(every(send2, 4), every(send2, 13))
    melt_sides = beside(every(send1, 10), every(send2, 3))
    store_sides = beside(every(send1, 0), every(send1, 9))
    store_moved = jnp.where(
        lanes < 64, pltpu.roll(store_sides, 4, 1), pltpu.roll(store_sides, LANES - 4, 1)
    )
    send2[pl.ds(15, TILES, stride=MSG), :] = jnp.where(
        jnp.logical_or(lanes < 4, lanes >= LANES - 4), melt_sides, store_moved
    )
    own2 = to_all(send2, recv2, 3, 1)

    chan_low.wait_recv()
    chan_high.wait_recv()
    low_side = jnp.where(jnp.logical_and(lanes >= LANES - 4, a > 0), cond_low[...], 0.0)
    cond[EDGE : EDGE + TILES, RUN * LANES :] = jnp.where(
        jnp.logical_and(lanes < 4, a < TILES - 1), cond_high[...], low_side
    )
    chan_up = post(cond.at[pl.ds(EDGE, EDGE)], cond.at[pl.ds(EDGE + TILES, EDGE)], 4, {"grp": up})
    chan_down = post(cond.at[pl.ds(TILES, EDGE)], cond.at[pl.ds(0, EDGE)], 5, {"grp": down})

    def rows_beside(buffer, number):
        first = post(
            buffer.at[pl.ds(EDGE * MSG, 4 * MSG)], buffer.at[pl.ds((EDGE + TILES) * MSG, 4 * MSG)], number, {"grp": up}
        )
        second = post(
            buffer.at[pl.ds((TILES + 4) * MSG, 4 * MSG)], buffer.at[pl.ds(4 * MSG, 4 * MSG)], number + 1, {"grp": down}
        )
        return first, second

    others = (TILES - 1) * MSG
    own1.wait()
    all_done(recv1, others, recv_sem.at[2])
    rows1 = rows_beside(recv1, 6)
    chan_up.wait_recv()
    chan_down.wait_recv()
    for copy in rows1:
        copy.wait_recv()

    row = lax.broadcasted_iota(jnp.int32, (TALL, LANES), 0)
    inside = jnp.logical_and(
        jnp.logical_or(row >= EDGE, g > 0), jnp.logical_or(row < EDGE + TILES, g < GROUP - 1)
    )

    def mesh_rows(ref, k):
        return ref[pl.ds(k, TALL, stride=MSG), :]

    for k in range(RUN):
        at = slice(k * LANES, (k + 1) * LANES)
        coef[:, at] = jnp.where(inside, cond[:, at] / (1.0 + mesh_rows(recv1, k)), 0.0)

    own2.wait()
    all_done(recv2, others, recv_sem.at[3])
    rows2 = rows_beside(recv2, 8)
    for copy in rows2:
        copy.wait_recv()

    side = mesh_rows(recv2, 15)
    lane_tall = lax.broadcasted_iota(jnp.int32, (TALL, LANES), 1)
    store_side = jnp.where(lane_tall < 64, pltpu.roll(side, LANES - 4, 1), pltpu.roll(side, 4, 1))
    used = jnp.logical_or(lane_tall < 4, lane_tall >= LANES - 4)
    store_side = jnp.where(used, store_side, 0.0)
    melt_side = jnp.where(used, side, 0.0)
    at = slice(RUN * LANES, WIDE)
    coef[:, at] = jnp.where(inside, cond[:, at] / (1.0 + store_side), 0.0)
    melts = [mesh_rows(recv1, RUN + k) for k in range(MSG - RUN)]
    melts += [mesh_rows(recv2, k) for k in range(2 * RUN - MSG)] + [melt_side]
    keeps = [1.0 - melt_rate * part for part in melts]
    now = [jnp.where(inside, mesh_rows(recv2, 2 * RUN - MSG + k), 0.0) for k in range(RUN + 1)]
    keep = jnp.concatenate(keeps, axis=1)
    field = jnp.concatenate(now, axis=1)
    pressure[...] = field
    for sweep in range(HSWEEPS):
        field = pressure[...]
        rate = coef[...]
        sides = (
            pltpu.roll(field, 1, 1) + pltpu.roll(field, WIDE - 1, 1) + pltpu.roll(field, 1, 0) + pltpu.roll(field, TALL - 1, 0)
        )
        pressure[...] = keep * field + rate * (sides - 4.0 * field)

    for k in range(RUN):
        for i in range(TILES // 8):
            cells = pressure[EDGE + 8 * i : EDGE + 8 * i + 8, k * LANES : (k + 1) * LANES]
            back_send[pl.ds(8 * i * MSG + k, 8, stride=MSG), :] = cells
    press_out[...] = pressure[EDGE : EDGE + TILES, : RUN * LANES]
    press_copy = pltpu.make_async_copy(press_out, press_hbm, out_sem.at[0])
    press_copy.start()

    pad0 = LEVELS[0][1]

    def give_back(d, carry):
        target = lax.rem(a + d, TILES)
        post(
            back_send.at[rows_at(target * MSG, MSG)], lev0.at[a, pl.ds(pad0, MSG)], 10, {"col": target}
        )
        return carry

    lax.fori_loop(1, TILES, give_back, 0)
    own_back = pltpu.make_async_copy(
        back_send.at[rows_at(a * MSG, MSG)], lev0.at[a, pl.ds(pad0, MSG)], self_sem.at[2]
    )
    own_back.start()
    own_back.wait()
    all_done(back_send, others, recv_sem.at[10])

    levels = (lev0, lev1, lev2, lev3, lev4)
    for level, (nodes, pad, tall) in enumerate(LEVELS):
        ref = levels[level]
        index = lax.broadcasted_iota(jnp.int32, (tall, LANES), 0) * LANES + lax.broadcasted_iota(
            jnp.int32, (tall, LANES), 1
        )
        for node in range(nodes // 2):
            begin = starts[(2 * node) << level]
            length = jnp.clip(starts[(2 * node + 1) << level] - begin, 0, (RUN << level) * LANES)
            first = lax.shift_right_logical(length, 7)
            turn = lax.bitwise_and(length, LANES - 1)
            mine_rows = ref[2 * node, pl.ds(pad, tall), :]
            here = pltpu.roll(ref[2 * node + 1, pl.ds(pad - first, tall), :], turn, 1)
            before = pltpu.roll(ref[2 * node + 1, pl.ds(pad - 1 - first, tall), :], turn, 1)
            moved = jnp.where(lane >= turn, here, before)
            merged = jnp.where(index < length, mine_rows, moved)
            if level < len(LEVELS) - 1:
                levels[level + 1][node, pl.ds(LEVELS[level + 1][1], tall), :] = merged
            else:
                value = thaw[...].astype(jnp.float32) * fric[...] * (basal[...] + merged)
                sens[...] = value

    sens_copy = pltpu.make_async_copy(sens, sens_hbm, out_sem.at[1])
    sens_copy.start()

    parts = []
    for q in range(PARTS):
        for d in range(1, CHIPS):
            same_core = lax.rem(chip + d, CHIPS) * 2 + core
            copy = pltpu.make_async_remote_copy(
                src_ref=sens.at[pl.ds(q * PART, PART)],
                dst_ref=gathered.at[d, pl.ds(q * PART, PART)],
                send_sem=part_send.at[q, d - 1],
                recv_sem=part_recv.at[q, d - 1],
                device_id={"grp": same_core},
                device_id_type=MESH,
            )
            copy.start()
            parts.append(copy)

    def factor(who, d):
        return mix_ref[who, lax.rem(chip + CHIPS - d, CHIPS) * 2 + core]

    to_self = [factor(g, d) for d in range(CHIPS)]
    to_other = [factor(sibling, d) for d in range(CHIPS)]
    pairs = []
    for q in range(PARTS):
        at = pl.ds(q * PART, PART)
        for d in range(CHIPS - 1):
            parts[q * (CHIPS - 1) + d].wait_recv()
        pieces = [sens[at, :]] + [gathered[d, at, :] for d in range(1, CHIPS)]
        other_send[at, :] = sum(to_other[d] * pieces[d] for d in range(CHIPS))
        copy = pltpu.make_async_remote_copy(
            src_ref=other_send.at[at], dst_ref=other_recv.at[at], send_sem=pair_send.at[q], recv_sem=pair_recv.at[q],
            device_id={"grp": sibling}, device_id_type=MESH,
        )
        copy.start()
        pairs.append(copy)
        mine[at, :] = sum(to_self[d] * pieces[d] for d in range(CHIPS))

    map_load.wait()
    total = jnp.zeros((CONTROLS, LANES), jnp.float32)
    for q in range(PARTS):
        pairs[q].wait_recv()

        def product(j, total):
            at = rows_at(j * 8, 8)
            mixed = (mine[at, :] + other_recv[at, :]).astype(jnp.bfloat16).astype(jnp.float32)
            for s in range(8):
                block = cmap[:, pl.ds(pl.multiple_of(j * 1024 + s * LANES, LANES), LANES)]
                total = total + block.astype(jnp.float32) * mixed[s : s + 1, :]
            return total

        total = lax.fori_loop(q * PART // 8, (q + 1) * PART // 8, product, total)
    grad_ref[...] = jnp.sum(total.T, axis=0, keepdims=True)

    chan_low.wait_send()
    chan_high.wait_send()
    chan_up.wait_send()
    chan_down.wait_send()
    for copy in rows1 + rows2:
        copy.wait_send()
    all_done(send1, others, send_sem.at[2])
    all_done(send2, others, send_sem.at[3])
    all_done(back_send, others, send_sem.at[10])
    for copy in parts + pairs:
        copy.wait_send()
    press_copy.wait()
    sens_copy.wait()


def on_device(
    velocity_cotangent,
    vertical_inverse,
    sliding_speed,
    friction_coef,
    thawed_bed,
    basal_melt,
    storage_coef,
    owner_tile,
    channel_open,
    group_mix,
    control_map,
):
    adjoint = jnp.dot(
        vertical_inverse.T,
        velocity_cotangent,
        precision=lax.Precision.HIGHEST,
        preferred_element_type=jnp.float32,
    )
    shaped = [x.reshape(ROWS, LANES) for x in (sliding_speed, friction_coef, thawed_bed, basal_melt, storage_coef, owner_tile)]
    f32 = jnp.float32
    anywhere = pl.BlockSpec(memory_space=pl.ANY)
    vmem = pl.BlockSpec(memory_space=pltpu.VMEM)
    columns = pltpu.VMEM((ROWS, LANES), f32)
    padded = pltpu.VMEM((ROWS + 24, LANES), f32)
    numbers = pltpu.VMEM((ROWS, LANES), jnp.int32)
    messages = pltpu.VMEM(((TILES + 1) * MSG, LANES), f32)
    received = pltpu.VMEM(((TALL + 1) * MSG, LANES), f32)
    field = pltpu.VMEM((TALL, WIDE), f32)
    dma = pltpu.SemaphoreType.DMA
    pressure, sensitivity, gradient = pl.pallas_call(
        kernel,
        out_shape=(
            jax.ShapeDtypeStruct((TILES, RUN * LANES), f32),
            jax.ShapeDtypeStruct((ROWS, LANES), f32),
            jax.ShapeDtypeStruct((1, CONTROLS), f32),
        ),
        in_specs=[pl.BlockSpec(memory_space=pltpu.SMEM), vmem] + [anywhere] * 9,
        out_specs=(anywhere, anywhere, vmem),
        scratch_shapes=[
            pltpu.VMEM((LAYERS, COLUMNS), f32),
            pltpu.VMEM((CONTROLS, COLUMNS), jnp.bfloat16),
            columns, columns, numbers, padded, padded, numbers,
            pltpu.VMEM((TILES, RUN * LANES), jnp.int32),
            padded, columns,
            messages, messages, received, received,
            field, pltpu.VMEM((TILES, LANES), f32), pltpu.VMEM((TILES, LANES), f32),
            field, field, pltpu.VMEM((TILES, RUN * LANES), f32), messages,
        ]
        + [pltpu.VMEM((nodes, pad + tall, LANES), f32) for nodes, pad, tall in LEVELS]
        + [
            columns, pltpu.VMEM((CHIPS, ROWS, LANES), f32), columns, columns, columns,
            dma((8,)), dma((PARTS,)), dma((3,)), dma((11,)), dma((11,)),
            dma((PARTS, CHIPS - 1)), dma((PARTS, CHIPS - 1)), dma((PARTS,)), dma((PARTS,)), dma((2,)),
        ],
        compiler_params=pltpu.CompilerParams(
            collective_id=0, has_side_effects=True, vmem_limit_bytes=48 * 1024 * 1024
        ),
    )(group_mix, vertical_inverse, velocity_cotangent, *shaped, channel_open, control_map)
    return adjoint, pressure, sensitivity.reshape(COLUMNS), gradient.reshape(CONTROLS)


def solution(mesh):
    in_specs = (
        P(None, ("col", "grp")),
        P(),
        P(("col", "grp")),
        P(("col", "grp")),
        P(("col", "grp")),
        P(("col", "grp")),
        P(("col", "grp")),
        P(("col", "grp"), None),
        P("grp", "col"),
        P(),
        P(("col", "grp"), None),
    )
    out_specs = (P(None, ("col", "grp")), P("grp", "col"), P(("col", "grp")), P(("col", "grp")))
    return jax.shard_map(
        on_device, mesh=mesh, in_specs=in_specs, out_specs=out_specs, check_vma=False
    )
```

time: 614 us -> 69.2 us (0.11); the launches traced: 606 us -> 68.9 us
  loops' own time: 186 us -> 0 us
  local copies, waits for them, and re-layouts: 175 us -> 11.5 us
  other arithmetic: 85.7 us -> 0 us
  starting transfers between devices: 59.9 us -> 0 us
  Pallas kernels: 0 us -> 52.4 us
  waiting for transfers between devices: 48 us -> 0 us
  blocking collectives: 28.4 us -> 0 us
  between operations: 14.4 us -> 0.66 us
    another operation x2 -> x0, loops' own time: 186 us -> none  [the longest x1 125 us: on_device(): packed = lax.map(place_tile, tile_ids)]
    dynamic_slice x160 -> x0, local copies, waits for them, and re-layouts: 142 us -> none  [the longest x32 39.9 us: add_tile(): starts[tile]]
    pallas_call x0 -> x1, Pallas kernels: none -> 52.4 us  [on_device(): pl.pallas_call(kernel, out_shape=(jax.ShapeDtypeStruct((TILES, RUN * LANE...]
    ppermute x16 -> x0, starting transfers between devices: 50.3 us -> none  [the longest x8 32.1 us: extended(): lax.ppermute(lax.slice_in_dim(block, block.shape[dim] - width, None, axis...]
    dynamic_update_slice x32 -> x0, other arithmetic: 45.6 us -> none  [on_device(): packed = lax.map(place_tile, tile_ids)]
    all_to_all x1 -> x0, blocking collectives: 28.4 us -> none  [on_device(): lax.all_to_all(packed, 'col', split_axis=0, concat_axis=0, tiled=True)]
    all_gather x1 -> x0, waiting for transfers between devices: 23 us -> none  [on_device(): piece = lax.all_gather(sensitivity, 'grp', axis=0, tiled=True)]
    lt x32 -> x0, other arithmetic: 20.8 us -> none  [place_tile(): return jnp.where(slot_range[None, :] < counts[tile], window, 0.0)]
  transfers between devices with their start and end apart: 18 -> 0, of which waited for: 10 -> 0; matrix products, arithmetic and copies ran while one was open for 0% -> 0% of each run, Pallas kernels for 0% -> 0%
where the time goes in v1:
time: 69.2 us; the launch traced here: 68.9 us
  Pallas kernels  52.4 us (76%)
  local copies, waits for them, and re-layouts  11.5 us (17%)
  matrix products  4.36 us (6%)
    pallas_call x1, Pallas kernels, on_device(): pl.pallas_call(kernel, out_shape=(jax.ShapeDtypeStruct((TILES, RUN * LANE...  52.4 us
    unnamed x23, local copies, waits for them, and re-layouts  11.5 us
    dot_general x1, matrix products, on_device(): jnp.dot(vertical_inverse.T, velocity_cotangent, precision=lax.Precision.H...  4.36 us

profile of v1, /device:TPU:1, one launch (start us, length us, event | category | flops | bytes accessed | tf_op | source)
XLA Modules:
  0.0 68.9 jit_solution(9899761677281079371)
XLA Ops:
  0.6 0.0 copy-start
  0.6 1.9 %copy-done = f32[20,32768]{1,0:T(8,128)S(1)} copy-done((f32[20,32768]{1,0:T(8,128)S(1)}, f32[20,32768]{1,0:T(8,128)}, u32[]{:S(2)}) %copy-start) | copy-done | bytes 2621464
  2.5 0.0 copy-start.1
  2.5 0.9 %copy-done.1 = s32[32,1280]{1,0:T(8,128)S(1)} copy-done((s32[32,1280]{1,0:T(8,128)S(1)}, s32[32,1280]{1,0:T(8,128)}, u32[]{:S(2)}) %copy-start.1) | copy-done | bytes 163864
  3.4 0.0 copy-start.2
  3.4 0.9 %copy-done.2 = f32[32768]{0:T(1024)S(1)} copy-done((f32[32768]{0:T(1024)S(1)}, f32[32768]{0:T(1024)}, u32[]{:S(2)}) %copy-start.2) | copy-done | bytes 131096
  4.3 0.0 copy-start.3
  4.3 0.9 %copy-done.3 = f32[32768]{0:T(1024)S(1)} copy-done((f32[32768]{0:T(1024)S(1)}, f32[32768]{0:T(1024)}, u32[]{:S(2)}) %copy-start.3) | copy-done | bytes 131096
  5.3 0.0 copy-start.4
  5.3 0.9 %copy-done.4 = s32[32768]{0:T(1024)S(1)} copy-done((s32[32768]{0:T(1024)S(1)}, s32[32768]{0:T(1024)}, u32[]{:S(2)}) %copy-start.4) | copy-done | bytes 131096
  6.2 0.0 copy-start.5
  6.2 0.9 %copy-done.5 = f32[32768]{0:T(1024)S(1)} copy-done((f32[32768]{0:T(1024)S(1)}, f32[32768]{0:T(1024)}, u32[]{:S(2)}) %copy-start.5) | copy-done | bytes 131096
  7.1 0.0 copy-start.6
  7.1 0.9 %copy-done.6 = f32[32768]{0:T(1024)S(1)} copy-done((f32[32768]{0:T(1024)S(1)}, f32[32768]{0:T(1024)}, u32[]{:S(2)}) %copy-start.6) | copy-done | bytes 131096
  8.0 0.0 copy-start.7
  8.0 0.9 %copy-done.7 = s32[32768,1]{0,1:T(1,128)S(1)} copy-done((s32[32768,1]{0,1:T(1,128)S(1)}, s32[32768,1]{0,1:T(1,128)}, u32[]{:S(2)}) %copy-start.7) | copy-done | bytes 131096
  8.9 0.0 copy-start.8
  8.9 0.7 %copy-done.8 = f32[20,20]{1,0:T(8,128)S(1)} copy-done((f32[20,20]{1,0:T(8,128)S(1)}, f32[20,20]{1,0:T(8,128)}, u32[]{:S(2)}) %copy-start.8) | copy-done | bytes 1624
  9.6 0.0 copy-start.9
  9.6 0.7 copy-done.9
  10.3 52.4 %shard_map.138 = (f32[32,1280]{1,0:T(8,128)S(1)}, f32[256,128]{1,0:T(8,128)S(1)}, f32[1,64]{1,0:T(1,128)S(1)}) custom-call(f32[8,8]{1,0:T(8,128)S(1)} %copy-done.9, f32[20,20]{1,0:T(8,128)S(1)} %copy-done.8, f32[20,32768]{1,0:T(8,128)S(1)} %copy-done, f32[256,128]{1,0:T(8,128)S(1)} %bitcast.10, f32[256,128]{1,0:T(8,128)S(1)} %bitcast.11, ...), custom_call_target="tpu_custom_call" | custom-call | tf_op jit(solution)/shard_map/pallas_call | solution.py:422
  62.7 4.4 %fusion = f32[20,32768]{1,0:T(8,128)} fusion(f32[20,20]{1,0:T(8,128)S(1)} %copy-done.8, f32[20,32768]{1,0:T(8,128)S(1)} %copy-done), kind=kOutput, calls=%fused_computation | convolution fusion | flops 157286400 | bytes 5244480 | tf_op jit(solution)/shard_map/dot_general | solution.py:405
  67.1 0.7 copy.18
  67.7 0.7 copy.19
  68.4 0.5 copy.20
Async XLA Ops:
  0.6 1.9 %copy-start = (f32[20,32768]{1,0:T(8,128)S(1)}, f32[20,32768]{1,0:T(8,128)}, u32[]{:S(2)}) copy-start(f32[20,32768]{1,0:T(8,128)} %cot_hbm.1) | copy-start | bytes 7864324
  2.5 0.9 %copy-start.1 = (s32[32,1280]{1,0:T(8,128)S(1)}, s32[32,1280]{1,0:T(8,128)}, u32[]{:S(2)}) copy-start(s32[32,1280]{1,0:T(8,128)} %open_hbm.1) | copy-start | bytes 491524
  3.4 0.9 %copy-start.2 = (f32[32768]{0:T(1024)S(1)}, f32[32768]{0:T(1024)}, u32[]{:S(2)}) copy-start(f32[32768]{0:T(1024)} %param.13) | copy-start | bytes 393220
  4.3 0.9 %copy-start.3 = (f32[32768]{0:T(1024)S(1)}, f32[32768]{0:T(1024)}, u32[]{:S(2)}) copy-start(f32[32768]{0:T(1024)} %param.14) | copy-start | bytes 393220
  5.3 0.9 %copy-start.4 = (s32[32768]{0:T(1024)S(1)}, s32[32768]{0:T(1024)}, u32[]{:S(2)}) copy-start(s32[32768]{0:T(1024)} %param.15) | copy-start | bytes 393220
  6.2 0.9 %copy-start.5 = (f32[32768]{0:T(1024)S(1)}, f32[32768]{0:T(1024)}, u32[]{:S(2)}) copy-start(f32[32768]{0:T(1024)} %param.16) | copy-start | bytes 393220
  7.1 0.9 %copy-start.6 = (f32[32768]{0:T(1024)S(1)}, f32[32768]{0:T(1024)}, u32[]{:S(2)}) copy-start(f32[32768]{0:T(1024)} %param.17) | copy-start | bytes 393220
  8.0 0.9 %copy-start.7 = (s32[32768,1]{0,1:T(1,128)S(1)}, s32[32768,1]{0,1:T(1,128)}, u32[]{:S(2)}) copy-start(s32[32768,1]{0,1:T(1,128)} %param.18) | copy-start | bytes 393220
  8.9 0.7 %copy-start.8 = (f32[20,20]{1,0:T(8,128)S(1)}, f32[20,20]{1,0:T(8,128)}, u32[]{:S(2)}) copy-start(f32[20,20]{1,0:T(8,128)} %inverse_ref.1) | copy-start | bytes 4804
  9.6 0.7 copy-start.9

commit v2 on v1

--- a/solution.py
+++ b/solution.py
@@ -1,3 +1,5 @@
+import functools
+
 import jax
 import jax.numpy as jnp
 from jax import lax
@@ -25,6 +27,7 @@
 PARTS = 4
 PART = ROWS // PARTS
 MESH = pl.DeviceIdType.MESH
+VMEM_BYTES = 64 * 1024 * 1024
 
 LEVELS = ((32, 16, 24), (16, 24, 40), (8, 48, 80), (4, 88, 160), (2, 168, 256))
 
@@ -286,17 +289,17 @@
     def give_back(d, carry):
         target = lax.rem(a + d, TILES)
         post(
-            back_send.at[rows_at(target * MSG, MSG)], lev0.at[a, pl.ds(pad0, MSG)], 10, {"col": target}
+            back_send.at[rows_at(target * MSG, RUN)], lev0.at[a, pl.ds(pad0, RUN)], 10, {"col": target}
         )
         return carry
 
     lax.fori_loop(1, TILES, give_back, 0)
     own_back = pltpu.make_async_copy(
-        back_send.at[rows_at(a * MSG, MSG)], lev0.at[a, pl.ds(pad0, MSG)], self_sem.at[2]
+        back_send.at[rows_at(a * MSG, RUN)], lev0.at[a, pl.ds(pad0, RUN)], self_sem.at[2]
     )
     own_back.start()
     own_back.wait()
-    all_done(back_send, others, recv_sem.at[10])
+    all_done(back_send, (TILES - 1) * RUN, recv_sem.at[10])
 
     levels = (lev0, lev1, lev2, lev3, lev4)
     for level, (nodes, pad, tall) in enumerate(LEVELS):
@@ -382,11 +385,48 @@
         copy.wait_send()
     all_done(send1, others, send_sem.at[2])
     all_done(send2, others, send_sem.at[3])
-    all_done(back_send, others, send_sem.at[10])
+    all_done(back_send, (TILES - 1) * RUN, send_sem.at[10])
     for copy in parts + pairs:
         copy.wait_send()
     press_copy.wait()
     sens_copy.wait()
+
+
+def adjoint_kernel(
+    inverse_ref, cot_hbm, press_in, sens_in, grad_in,
+    adj_hbm, press_out, sens_out, grad_out,
+    cot, adj, in_sem, out_sem, pass_sem,
+):
+    pieces = in_sem.shape[0]
+    width = COLUMNS // pieces
+    ins, outs = [], []
+    for q in range(pieces):
+        at = pl.ds(q * width, width)
+        copy = pltpu.make_async_copy(cot_hbm.at[:, at], cot.at[:, at], in_sem.at[q])
+        copy.start()
+        ins.append(copy)
+    for number, (src, dst) in enumerate(((press_in, press_out), (sens_in, sens_out), (grad_in, grad_out))):
+        copy = pltpu.make_async_copy(src, dst, pass_sem.at[number])
+        copy.start()
+        outs.append(copy)
+    matrix = inverse_ref[...].T
+    high = matrix.astype(jnp.bfloat16)
+    low = (matrix - high.astype(jnp.float32)).astype(jnp.bfloat16)
+    dot = functools.partial(jnp.dot, preferred_element_type=jnp.float32)
+    for q in range(pieces):
+        ins[q].wait()
+        for start in range(q * width, (q + 1) * width, 1024):
+            at = slice(start, start + 1024)
+            values = cot[:, at]
+            values_high = values.astype(jnp.bfloat16)
+            values_low = (values - values_high.astype(jnp.float32)).astype(jnp.bfloat16)
+            adj[:, at] = dot(high, values_high) + (dot(high, values_low) + dot(low, values_high))
+        at = pl.ds(q * width, width)
+        copy = pltpu.make_async_copy(adj.at[:, at], adj_hbm.at[:, at], out_sem.at[q])
+        copy.start()
+        outs.append(copy)
+    for copy in outs:
+        copy.wait()
 
 
 def on_device(
@@ -402,15 +442,9 @@
     group_mix,
     control_map,
 ):
-    adjoint = jnp.dot(
-        vertical_inverse.T,
-        velocity_cotangent,
-        precision=lax.Precision.HIGHEST,
-        preferred_element_type=jnp.float32,
-    )
     shaped = [x.reshape(ROWS, LANES) for x in (sliding_speed, friction_coef, thawed_bed, basal_melt, storage_coef, owner_tile)]
     f32 = jnp.float32
-    anywhere = pl.BlockSpec(memory_space=pl.ANY)
+    anywhere = pl.BlockSpec(memory_space=pltpu.HBM)
     vmem = pl.BlockSpec(memory_space=pltpu.VMEM)
     columns = pltpu.VMEM((ROWS, LANES), f32)
     padded = pltpu.VMEM((ROWS + 24, LANES), f32)
@@ -445,9 +479,24 @@
             dma((PARTS, CHIPS - 1)), dma((PARTS, CHIPS - 1)), dma((PARTS,)), dma((PARTS,)), dma((2,)),
         ],
         compiler_params=pltpu.CompilerParams(
-            collective_id=0, has_side_effects=True, vmem_limit_bytes=48 * 1024 * 1024
+            collective_id=0, has_side_effects=True, vmem_limit_bytes=VMEM_BYTES
         ),
     )(group_mix, vertical_inverse, velocity_cotangent, *shaped, channel_open, control_map)
+    adjoint, pressure, sensitivity, gradient = pl.pallas_call(
+        adjoint_kernel,
+        out_shape=(
+            jax.ShapeDtypeStruct((LAYERS, COLUMNS), f32),
+            jax.ShapeDtypeStruct((TILES, RUN * LANES), f32),
+            jax.ShapeDtypeStruct((ROWS, LANES), f32),
+            jax.ShapeDtypeStruct((1, CONTROLS), f32),
+        ),
+        in_specs=[vmem] + [anywhere] * 4,
+        out_specs=(anywhere,) * 4,
+        scratch_shapes=[
+            pltpu.VMEM((LAYERS, COLUMNS), f32), pltpu.VMEM((LAYERS, COLUMNS), f32), dma((8,)), dma((8,)), dma((3,)),
+        ],
+        compiler_params=pltpu.CompilerParams(vmem_limit_bytes=VMEM_BYTES),
+    )(vertical_inverse, velocity_cotangent, pressure, sensitivity, gradient)
     return adjoint, pressure, sensitivity.reshape(COLUMNS), gradient.reshape(CONTROLS)
 
 

time: 69.2 us -> 61 us (0.88)
  local copies, waits for them, and re-layouts: 11.5 us -> 0 us
  Pallas kernels: 52.4 us -> 60.1 us
  matrix products: 4.36 us -> 0 us
    unnamed x23 -> x0, local copies, waits for them, and re-layouts: 11.5 us -> none
    pallas_call x0 -> x1, Pallas kernels: none -> 10.9 us  [on_device(): pl.pallas_call(adjoint_kernel, out_shape=(jax.ShapeDtypeStruct((LAYERS, C...]
    dot_general x1 -> x0, matrix products: 4.36 us -> none  [on_device(): jnp.dot(vertical_inverse.T, velocity_cotangent, precision=lax.Precision.H...]
    pallas_call x1, Pallas kernels: 52.4 us -> 49.2 us  [on_device(): pl.pallas_call(kernel, out_shape=(jax.ShapeDtypeStruct((TILES, RUN * LANE...]
where the time goes in v2:
time: 61 us; the launch traced here: 60.7 us
  Pallas kernels  60.1 us (99%)
  between operations  0.64 us (1%)
    pallas_call x1, Pallas kernels, on_device(): pl.pallas_call(kernel, out_shape=(jax.ShapeDtypeStruct((TILES, RUN * LANE...  49.2 us
    pallas_call x1, Pallas kernels, on_device(): pl.pallas_call(adjoint_kernel, out_shape=(jax.ShapeDtypeStruct((LAYERS, C...  10.9 us

profile of v2, /device:TPU:1, one launch (start us, length us, event | category | flops | bytes accessed | tf_op | source)
XLA Modules:
  0.0 60.7 jit_solution(16610504240823780852)
XLA Ops:
  0.6 49.2 %shard_map.138 = (f32[32,1280]{1,0:T(8,128)}, f32[256,128]{1,0:T(8,128)}, f32[1,64]{1,0:T(1,128)}) custom-call(f32[8,8]{1,0:T(8,128)} %mix_ref.1, f32[20,20]{1,0:T(8,128)} %inverse_ref.3, f32[20,32768]{1,0:T(8,128)} %cot_hbm.3, f32[256,128]{1,0:T(8,128)} %bitcast.8, f32[256,128]{1,0:T(8,128)} %bitcast.9, s32[256,128]{1,0:T(8,128)} %bitcast.10, ...), custom_call_target="tpu_custom_call" | custom-call | tf_op jit(solution)/shard_map/pallas_call | solution.py:456
  49.8 10.9 %shard_map.139 = (f32[20,32768]{1,0:T(8,128)}, f32[32,1280]{1,0:T(8,128)}, f32[256,128]{1,0:T(8,128)}, f32[1,64]{1,0:T(1,128)}) custom-call(f32[20,20]{1,0:T(8,128)} %inverse_ref.3, f32[20,32768]{1,0:T(8,128)} %cot_hbm.3, f32[32,1280]{1,0:T(8,128)} %get-tuple-element.11.press_in, f32[256,128]{1,0:T(8,128)} %get-tuple-element.12.sens_in, ...), custom_call_target="tpu_custom_call" | custom-call | tf_op jit(solution)/shard_map/pallas_call | solution.py:485

commit v3 on v2

--- a/solution.py
+++ b/solution.py
@@ -14,8 +14,10 @@
 TILES = 32
 GROUP = 8
 CHIPS = 4
+RING_Y, RING_Z = 4, 8
 COLUMNS = 32768
 LAYERS = 20
+LAYER_ROWS = 24
 LANES = 128
 ROWS = COLUMNS // LANES
 RUN = 10
@@ -24,6 +26,8 @@
 WIDE = RUN * LANES + LANES
 TALL = TILES + 2 * EDGE
 CONTROLS = 64
+PIECES = 4
+AHEAD = 4
 PARTS = 4
 PART = ROWS // PARTS
 MESH = pl.DeviceIdType.MESH
@@ -87,7 +91,7 @@
     lax.fori_loop(1, TILES, greet, 0)
     for other in (up, down):
         pl.semaphore_signal(barrier, inc=1, device_id={"grp": other}, device_id_type=MESH)
-    for d in range(1, CHIPS):
+    for d in (1, CHIPS - 1):
         same_core = lax.rem(chip + d, CHIPS) * 2 + core
         pl.semaphore_signal(barrier, inc=1, device_id={"grp": same_core}, device_id_type=MESH)
 
@@ -131,7 +135,7 @@
     chan_load.wait()
     cond[EDGE : EDGE + TILES, : RUN * LANES] = jnp.where(chan[...] == 1, diffusion_rate, 0.25 * diffusion_rate)
 
-    pl.semaphore_wait(barrier, TILES - 1 + 2 + CHIPS - 1)
+    pl.semaphore_wait(barrier, TILES - 1 + 2 + 2)
 
     def post(src, dst, number, where):
         copy = pltpu.make_async_remote_copy(
@@ -141,13 +145,21 @@
         copy.start()
         return copy
 
+    def outward(far, order):
+        return far + (1 - 2 * lax.rem(order, 2)) * ((order + 1) // 2)
+
+    def far_first(order):
+        away_z = outward(RING_Z // 2, order // RING_Y)
+        away_y = outward(RING_Y // 2, lax.rem(order, RING_Y))
+        return lax.rem(a // RING_Z + away_y, RING_Y) * RING_Z + lax.rem(a + away_z, RING_Z)
+
     def to_all(src, dst, number, self_number):
-        def one(d, carry):
-            target = lax.rem(a + d, TILES)
+        def one(order, carry):
+            target = far_first(order)
             post(src.at[rows_at(target * MSG, MSG)], dst.at[rows_at((EDGE + a) * MSG, MSG)], number, {"col": target})
             return carry
 
-        lax.fori_loop(1, TILES, one, 0)
+        lax.fori_loop(0, TILES - 1, one, 0)
         own = pltpu.make_async_copy(
             src.at[rows_at(a * MSG, MSG)], dst.at[rows_at((EDGE + a) * MSG, MSG)], self_sem.at[self_number]
         )
@@ -286,14 +298,14 @@
 
     pad0 = LEVELS[0][1]
 
-    def give_back(d, carry):
-        target = lax.rem(a + d, TILES)
+    def give_back(order, carry):
+        target = far_first(order)
         post(
             back_send.at[rows_at(target * MSG, RUN)], lev0.at[a, pl.ds(pad0, RUN)], 10, {"col": target}
         )
         return carry
 
-    lax.fori_loop(1, TILES, give_back, 0)
+    lax.fori_loop(0, TILES - 1, give_back, 0)
     own_back = pltpu.make_async_copy(
         back_send.at[rows_at(a * MSG, RUN)], lev0.at[a, pl.ds(pad0, RUN)], self_sem.at[2]
     )
@@ -326,31 +338,42 @@
     sens_copy = pltpu.make_async_copy(sens, sens_hbm, out_sem.at[1])
     sens_copy.start()
 
-    parts = []
+    def pass_on(q, slot, src, ahead):
+        copy = pltpu.make_async_remote_copy(
+            src_ref=src.at[pl.ds(q * PART, PART)],
+            dst_ref=gathered.at[slot, pl.ds(q * PART, PART)],
+            send_sem=part_send.at[q, slot - 1],
+            recv_sem=part_recv.at[q, slot - 1],
+            device_id={"grp": lax.rem(chip + ahead, CHIPS) * 2 + core},
+            device_id_type=MESH,
+        )
+        copy.start()
+        return copy
+
+    parts = {}
     for q in range(PARTS):
-        for d in range(1, CHIPS):
-            same_core = lax.rem(chip + d, CHIPS) * 2 + core
-            copy = pltpu.make_async_remote_copy(
-                src_ref=sens.at[pl.ds(q * PART, PART)],
-                dst_ref=gathered.at[d, pl.ds(q * PART, PART)],
-                send_sem=part_send.at[q, d - 1],
-                recv_sem=part_recv.at[q, d - 1],
-                device_id={"grp": same_core},
-                device_id_type=MESH,
-            )
-            copy.start()
-            parts.append(copy)
+        parts[q, 1] = pass_on(q, 1, sens, 1)
+        other = (q + PARTS // 2) % PARTS
+        parts[other, 3] = pass_on(other, 3, sens, CHIPS - 1)
+    in_order = []
+    for q in range(PARTS // 2):
+        other = q + PARTS // 2
+        parts[q, 1].wait_recv()
+        parts[q, 2] = pass_on(q, 2, gathered.at[1], 1)
+        parts[other, 3].wait_recv()
+        parts[other, 2] = pass_on(other, 2, gathered.at[3], CHIPS - 1)
+        in_order += [q, other]
 
     def factor(who, d):
         return mix_ref[who, lax.rem(chip + CHIPS - d, CHIPS) * 2 + core]
 
     to_self = [factor(g, d) for d in range(CHIPS)]
     to_other = [factor(sibling, d) for d in range(CHIPS)]
-    pairs = []
-    for q in range(PARTS):
+    pairs = {}
+    for q in in_order:
         at = pl.ds(q * PART, PART)
-        for d in range(CHIPS - 1):
-            parts[q * (CHIPS - 1) + d].wait_recv()
+        parts[q, 3 if q < PARTS // 2 else 1].wait_recv()
+        parts[q, 2].wait_recv()
         pieces = [sens[at, :]] + [gathered[d, at, :] for d in range(1, CHIPS)]
         other_send[at, :] = sum(to_other[d] * pieces[d] for d in range(CHIPS))
         copy = pltpu.make_async_remote_copy(
@@ -358,12 +381,12 @@
             device_id={"grp": sibling}, device_id_type=MESH,
         )
         copy.start()
-        pairs.append(copy)
+        pairs[q] = copy
         mine[at, :] = sum(to_self[d] * pieces[d] for d in range(CHIPS))
 
     map_load.wait()
     total = jnp.zeros((CONTROLS, LANES), jnp.float32)
-    for q in range(PARTS):
+    for q in in_order:
         pairs[q].wait_recv()
 
         def product(j, total):
@@ -386,7 +409,7 @@
     all_done(send1, others, send_sem.at[2])
     all_done(send2, others, send_sem.at[3])
     all_done(back_send, (TILES - 1) * RUN, send_sem.at[10])
-    for copy in parts + pairs:
+    for copy in list(parts.values()) + list(pairs.values()):
         copy.wait_send()
     press_copy.wait()
     sens_copy.wait()
@@ -395,36 +418,68 @@
 def adjoint_kernel(
     inverse_ref, cot_hbm, press_in, sens_in, grad_in,
     adj_hbm, press_out, sens_out, grad_out,
-    cot, adj, in_sem, out_sem, pass_sem,
+    cot, adj, press, sens, grad, in_sem, out_sem, pass_sem,
 ):
     pieces = in_sem.shape[0]
     width = COLUMNS // pieces
-    ins, outs = [], []
-    for q in range(pieces):
-        at = pl.ds(q * width, width)
-        copy = pltpu.make_async_copy(cot_hbm.at[:, at], cot.at[:, at], in_sem.at[q])
-        copy.start()
-        ins.append(copy)
-    for number, (src, dst) in enumerate(((press_in, press_out), (sens_in, sens_out), (grad_in, grad_out))):
+    outs, passes = [], []
+    for number, (src, dst) in enumerate(((press_in, press), (sens_in, sens), (grad_in, grad))):
         copy = pltpu.make_async_copy(src, dst, pass_sem.at[number])
         copy.start()
-        outs.append(copy)
+        passes.append(copy)
+    ins = [
+        pltpu.make_async_copy(
+            cot_hbm.at[:, pl.ds(q * width, width)], cot.at[:, pl.ds(q * width, width)], in_sem.at[q]
+        )
+        for q in range(pieces)
+    ]
+    for copy in ins[:AHEAD]:
+        copy.start()
+    tall = 8 * LAYER_ROWS
+    half = jnp.bfloat16
+    dot = functools.partial(jnp.dot, preferred_element_type=jnp.float32)
+    layer = lax.rem(lax.broadcasted_iota(jnp.int32, (tall, LAYERS), 0), LAYER_ROWS)
+    spread = (layer == lax.broadcasted_iota(jnp.int32, (tall, LAYERS), 1)).astype(jnp.float32).astype(half)
+    block = lax.broadcasted_iota(jnp.int32, (tall, tall), 0) // LAYER_ROWS
+    own_block = block == lax.broadcasted_iota(jnp.int32, (tall, tall), 1) // LAYER_ROWS
+
+    def diagonal(part):
+        rows = dot(spread, part).astype(half)
+        full = lax.dot_general(rows, spread, (((1,), (1,)), ((), ())), preferred_element_type=jnp.float32)
+        return jnp.where(own_block, full, 0.0).astype(half)
+
     matrix = inverse_ref[...].T
-    high = matrix.astype(jnp.bfloat16)
-    low = (matrix - high.astype(jnp.float32)).astype(jnp.bfloat16)
-    dot = functools.partial(jnp.dot, preferred_element_type=jnp.float32)
+    matrix_high = matrix.astype(half)
+    high = diagonal(matrix_high)
+    low = diagonal((matrix - matrix_high.astype(jnp.float32)).astype(half))
+    pad = jnp.zeros((LAYER_ROWS - LAYERS, 2 * LANES), jnp.float32)
+    step = 16 * LANES
     for q in range(pieces):
         ins[q].wait()
-        for start in range(q * width, (q + 1) * width, 1024):
-            at = slice(start, start + 1024)
-            values = cot[:, at]
-            values_high = values.astype(jnp.bfloat16)
-            values_low = (values - values_high.astype(jnp.float32)).astype(jnp.bfloat16)
-            adj[:, at] = dot(high, values_high) + (dot(high, values_low) + dot(low, values_high))
+        if q + AHEAD < pieces:
+            ins[q + AHEAD].start()
+        for start in range(q * width, (q + 1) * width, step):
+            tiles = []
+            for k in range(8):
+                tiles += [cot[:, start + 2 * k * LANES : start + 2 * (k + 1) * LANES], pad]
+            values = jnp.concatenate(tiles, axis=0)
+            values_high = values.astype(half)
+            values_low = (values - values_high.astype(jnp.float32)).astype(half)
+            result = dot(high, values_high) + (dot(high, values_low) + dot(low, values_high))
+            for k in range(8):
+                adj[:, start + 2 * k * LANES : start + 2 * (k + 1) * LANES] = result[
+                    k * LAYER_ROWS : k * LAYER_ROWS + LAYERS
+                ]
         at = pl.ds(q * width, width)
         copy = pltpu.make_async_copy(adj.at[:, at], adj_hbm.at[:, at], out_sem.at[q])
         copy.start()
         outs.append(copy)
+        if q == 0:
+            for number, (src, dst) in enumerate(((press, press_out), (sens, sens_out), (grad, grad_out))):
+                passes[number].wait()
+                copy = pltpu.make_async_copy(src, dst, pass_sem.at[number])
+                copy.start()
+                outs.append(copy)
     for copy in outs:
         copy.wait()
 
@@ -493,7 +548,9 @@
         in_specs=[vmem] + [anywhere] * 4,
         out_specs=(anywhere,) * 4,
         scratch_shapes=[
-            pltpu.VMEM((LAYERS, COLUMNS), f32), pltpu.VMEM((LAYERS, COLUMNS), f32), dma((8,)), dma((8,)), dma((3,)),
+            pltpu.VMEM((LAYERS, COLUMNS), f32), pltpu.VMEM((LAYERS, COLUMNS), f32),
+            pltpu.VMEM((TILES, RUN * LANES), f32), columns, pltpu.VMEM((1, CONTROLS), f32),
+            dma((PIECES,)), dma((PIECES,)), dma((3,)),
         ],
         compiler_params=pltpu.CompilerParams(vmem_limit_bytes=VMEM_BYTES),
     )(vertical_inverse, velocity_cotangent, pressure, sensitivity, gradient)

time: 61 us -> 54 us (0.89)
  Pallas kernels: 60.1 us -> 53.1 us
    pallas_call x1, Pallas kernels: 10.9 us -> 4.72 us  [on_device(): pl.pallas_call(adjoint_kernel, out_shape=(jax.ShapeDtypeStruct((LAYERS, C...]
    pallas_call x1, Pallas kernels: 49.2 us -> 48.4 us  [on_device(): pl.pallas_call(kernel, out_shape=(jax.ShapeDtypeStruct((TILES, RUN * LANE...]
where the time goes in v3:
time: 54 us; the launch traced here: 53.8 us
  Pallas kernels  53.1 us (98%)
  between operations  0.64 us (1%)
    pallas_call x1, Pallas kernels, on_device(): pl.pallas_call(kernel, out_shape=(jax.ShapeDtypeStruct((TILES, RUN * LANE...  48.4 us
    pallas_call x1, Pallas kernels, on_device(): pl.pallas_call(adjoint_kernel, out_shape=(jax.ShapeDtypeStruct((LAYERS, C...  4.72 us

profile of v3, /device:TPU:1, one launch (start us, length us, event | category | flops | bytes accessed | tf_op | source)
XLA Modules:
  0.0 53.8 jit_solution(7020274634216868833)
XLA Ops:
  0.6 48.4 %shard_map.138 = (f32[32,1280]{1,0:T(8,128)}, f32[256,128]{1,0:T(8,128)}, f32[1,64]{1,0:T(1,128)}) custom-call(f32[8,8]{1,0:T(8,128)} %mix_ref.1, f32[20,20]{1,0:T(8,128)} %inverse_ref.3, f32[20,32768]{1,0:T(8,128)} %cot_hbm.3, f32[256,128]{1,0:T(8,128)} %bitcast.8, f32[256,128]{1,0:T(8,128)} %bitcast.9, s32[256,128]{1,0:T(8,128)} %bitcast.10, ...), custom_call_target="tpu_custom_call" | custom-call | tf_op jit(solution)/shard_map/pallas_call | solution.py:511
  49.0 4.7 %shard_map.139 = (f32[20,32768]{1,0:T(8,128)}, f32[32,1280]{1,0:T(8,128)}, f32[256,128]{1,0:T(8,128)}, f32[1,64]{1,0:T(1,128)}) custom-call(f32[20,20]{1,0:T(8,128)} %inverse_ref.3, f32[20,32768]{1,0:T(8,128)} %cot_hbm.3, f32[32,1280]{1,0:T(8,128)} %get-tuple-element.11.press_in, f32[256,128]{1,0:T(8,128)} %get-tuple-element.12.sens_in, ...), custom_call_target="tpu_custom_call" | custom-call | tf_op jit(solution)/shard_map/pallas_call | solution.py:540

commit v4 on v3

--- a/solution.py
+++ b/solution.py
@@ -27,7 +27,6 @@
 TALL = TILES + 2 * EDGE
 CONTROLS = 64
 PIECES = 4
-AHEAD = 4
 PARTS = 4
 PART = ROWS // PARTS
 MESH = pl.DeviceIdType.MESH
@@ -42,11 +41,11 @@
 
 def kernel(
     mix_ref, inverse_ref, cot_hbm, slide_hbm, fric_hbm, thaw_hbm, melt_hbm, store_hbm, owner_hbm, open_hbm, map_hbm,
-    press_hbm, sens_hbm, grad_ref,
-    cot, cmap, slide, fric, thaw, melt, store, owner, chan, source, basal,
+    adj_hbm, press_hbm, sens_hbm, grad_ref,
+    cot, adj, cmap, slide, fric, thaw, melt, store, owner, chan, source, basal,
     send1, send2, recv1, recv2, cond, cond_low, cond_high, coef, pressure, press_out, back_send,
     lev0, lev1, lev2, lev3, lev4, sens, gathered, other_send, other_recv, mine,
-    load_sem, cot_sem, self_sem, send_sem, recv_sem, part_send, part_recv, pair_send, pair_recv, out_sem,
+    begins, load_sem, cot_sem, self_sem, send_sem, recv_sem, part_send, part_recv, pair_send, pair_recv, out_sem,
 ):
     a = lax.axis_index("col")
     g = lax.axis_index("grp")
@@ -66,20 +65,6 @@
     owner_load = load(owner_hbm, owner, 0)
     melt_load = load(melt_hbm, melt.at[pl.ds(0, ROWS)], 1)
     store_load = load(store_hbm, store.at[pl.ds(0, ROWS)], 2)
-    chan_load = load(open_hbm, chan, 3)
-    cot_loads = []
-    piece = COLUMNS // PARTS
-    for q in range(PARTS):
-        copy = pltpu.make_async_copy(
-            cot_hbm.at[:, pl.ds(q * piece, piece)], cot.at[:, pl.ds(q * piece, piece)], cot_sem.at[q]
-        )
-        copy.start()
-        cot_loads.append(copy)
-    thaw_load = load(thaw_hbm, thaw, 4)
-    slide_load = load(slide_hbm, slide, 5)
-    fric_load = load(fric_hbm, fric, 6)
-    map_load = load(map_hbm, cmap, 7)
-
     barrier = pltpu.get_barrier_semaphore()
 
     def greet(d, carry):
@@ -94,6 +79,20 @@
     for d in (1, CHIPS - 1):
         same_core = lax.rem(chip + d, CHIPS) * 2 + core
         pl.semaphore_signal(barrier, inc=1, device_id={"grp": same_core}, device_id_type=MESH)
+
+    cot_loads = []
+    piece = COLUMNS // PARTS
+    for q in range(PARTS):
+        copy = pltpu.make_async_copy(
+            cot_hbm.at[:, pl.ds(q * piece, piece)], cot.at[:, pl.ds(q * piece, piece)], cot_sem.at[q]
+        )
+        copy.start()
+        cot_loads.append(copy)
+    chan_load = load(open_hbm, chan, 3)
+    thaw_load = load(thaw_hbm, thaw, 4)
+    slide_load = load(slide_hbm, slide, 5)
+    fric_load = load(fric_hbm, fric, 6)
+    map_load = load(map_hbm, cmap, 7)
 
     lane = lax.broadcasted_iota(jnp.int32, (1, LANES), 1)
     edge_rows = jnp.zeros((4 * MSG, LANES), jnp.float32)
@@ -109,33 +108,21 @@
         partial = jnp.sum(below.reshape(ROWS // 8, 8, LANES), axis=0)
         starts.append(jnp.clip(jnp.sum(partial).astype(jnp.int32), 0, COLUMNS))
     starts.append(jnp.int32(COLUMNS))
+    for t in range(TILES + 1):
+        begins[t] = starts[t]
 
     slot = lax.broadcasted_iota(jnp.int32, (MSG, LANES), 0) * LANES + lax.broadcasted_iota(
         jnp.int32, (MSG, LANES), 1
     )
 
-    def window(ref, t):
-        first = lax.shift_right_logical(starts[t], 7)
-        turn = lax.bitwise_and(starts[t], LANES - 1)
+    def window(ref, begin, end):
+        first = lax.shift_right_logical(begin, 7)
+        turn = lax.bitwise_and(begin, LANES - 1)
         back_turn = lax.bitwise_and(LANES - turn, LANES - 1)
         low = pltpu.roll(ref[pl.ds(first, MSG), :], back_turn, 1)
         high = pltpu.roll(ref[pl.ds(first + 1, MSG), :], back_turn, 1)
         both = jnp.where(lane < LANES - turn, low, high)
-        return jnp.where(slot < starts[t + 1] - starts[t], both, 0.0)
-
-    store_load.wait()
-    melt_load.wait()
-    for t in range(TILES):
-        stored = window(store, t)
-        melted = window(melt, t)
-        send1[MSG * t : MSG * t + RUN, :] = stored[:RUN]
-        send1[MSG * t + RUN : MSG * (t + 1), :] = melted[: MSG - RUN]
-        send2[MSG * t : MSG * t + 2 * RUN - MSG, :] = melted[MSG - RUN : RUN]
-
-    chan_load.wait()
-    cond[EDGE : EDGE + TILES, : RUN * LANES] = jnp.where(chan[...] == 1, diffusion_rate, 0.25 * diffusion_rate)
-
-    pl.semaphore_wait(barrier, TILES - 1 + 2 + 2)
+        return jnp.where(slot < end - begin, both, 0.0)
 
     def post(src, dst, number, where):
         copy = pltpu.make_async_remote_copy(
@@ -145,12 +132,19 @@
         copy.start()
         return copy
 
+    def keep_own(src, dst, self_number):
+        own = pltpu.make_async_copy(
+            src.at[rows_at(a * MSG, MSG)], dst.at[rows_at((EDGE + a) * MSG, MSG)], self_sem.at[self_number]
+        )
+        own.start()
+        return own
+
     def outward(far, order):
-        return far + (1 - 2 * lax.rem(order, 2)) * ((order + 1) // 2)
+        return far + (1 - 2 * (order % 2)) * ((order + 1) // 2)
 
     def far_first(order):
         away_z = outward(RING_Z // 2, order // RING_Y)
-        away_y = outward(RING_Y // 2, lax.rem(order, RING_Y))
+        away_y = outward(RING_Y // 2, order % RING_Y)
         return lax.rem(a // RING_Z + away_y, RING_Y) * RING_Z + lax.rem(a + away_z, RING_Z)
 
     def to_all(src, dst, number, self_number):
@@ -160,18 +154,32 @@
             return carry
 
         lax.fori_loop(0, TILES - 1, one, 0)
-        own = pltpu.make_async_copy(
-            src.at[rows_at(a * MSG, MSG)], dst.at[rows_at((EDGE + a) * MSG, MSG)], self_sem.at[self_number]
-        )
-        own.start()
-        return own
+        return keep_own(src, dst, self_number)
 
     def all_done(buffer, rows, sem):
         pltpu.make_async_copy(buffer.at[pl.ds(0, rows)], buffer.at[pl.ds(0, rows)], sem).wait()
 
+    store_load.wait()
+    melt_load.wait()
+    for group in range(TILES // 8):
+        targets = [far_first(order) for order in range(group * 8, (group + 1) * 8)]
+        for t in targets:
+            at = pl.multiple_of(t * MSG, MSG)
+            begin, end = begins[t], begins[t + 1]
+            stored = window(store, begin, end)
+            melted = window(melt, begin, end)
+            send1[pl.ds(at, RUN), :] = stored[:RUN]
+            send1[pl.ds(at + RUN, MSG - RUN), :] = melted[: MSG - RUN]
+            send2[pl.ds(at, 2 * RUN - MSG), :] = melted[MSG - RUN : RUN]
+        if group == 0:
+            pl.semaphore_wait(barrier, TILES - 1 + 2 + 2)
+        for t in targets[: TILES - 1 - group * 8]:
+            post(send1.at[rows_at(t * MSG, MSG)], recv1.at[rows_at((EDGE + a) * MSG, MSG)], 2, {"col": t})
+    own1 = keep_own(send1, recv1, 0)
+    chan_load.wait()
+    cond[EDGE : EDGE + TILES, : RUN * LANES] = jnp.where(chan[...] == 1, diffusion_rate, 0.25 * diffusion_rate)
     chan_low = post(cond.at[EDGE : EDGE + TILES, (RUN - 1) * LANES : RUN * LANES], cond_low, 0, {"col": right})
     chan_high = post(cond.at[EDGE : EDGE + TILES, 0:LANES], cond_high, 1, {"col": left})
-    own1 = to_all(send1, recv1, 2, 0)
 
     weight = jnp.broadcast_to(inverse_ref[:, LAYERS - 1 : LAYERS], (LAYERS, LANES))
     sublane = lax.broadcasted_iota(jnp.int32, (8, LANES), 0)
@@ -196,7 +204,7 @@
         lax.fori_loop(q * 8, (q + 1) * 8, last_layer, 0)
 
     for t in range(TILES):
-        send2[MSG * t + 2 * RUN - MSG : MSG * t + 3 * RUN - MSG, :] = window(source, t)[:RUN]
+        send2[MSG * t + 2 * RUN - MSG : MSG * t + 3 * RUN - MSG, :] = window(source, starts[t], starts[t + 1])[:RUN]
 
     tile = lax.broadcasted_iota(jnp.int32, (TILES, LANES), 0)
     lanes = lax.broadcasted_iota(jnp.int32, (TILES, LANES), 1)
@@ -219,6 +227,45 @@
         jnp.logical_or(lanes < 4, lanes >= LANES - 4), melt_sides, store_moved
     )
     own2 = to_all(send2, recv2, 3, 1)
+
+    tall = 8 * LAYER_ROWS
+    half = jnp.bfloat16
+    dot = functools.partial(jnp.dot, preferred_element_type=jnp.float32)
+    layer = lax.rem(lax.broadcasted_iota(jnp.int32, (tall, LAYERS), 0), LAYER_ROWS)
+    spread = (layer == lax.broadcasted_iota(jnp.int32, (tall, LAYERS), 1)).astype(jnp.float32).astype(half)
+    block = lax.broadcasted_iota(jnp.int32, (tall, tall), 0) // LAYER_ROWS
+    own_block = block == lax.broadcasted_iota(jnp.int32, (tall, tall), 1) // LAYER_ROWS
+
+    def diagonal(part):
+        rows = dot(spread, part).astype(half)
+        full = lax.dot_general(rows, spread, (((1,), (1,)), ((), ())), preferred_element_type=jnp.float32)
+        return jnp.where(own_block, full, 0.0).astype(half)
+
+    matrix = inverse_ref[...].T
+    matrix_high = matrix.astype(half)
+    high = diagonal(matrix_high)
+    low = diagonal((matrix - matrix_high.astype(jnp.float32)).astype(half))
+    pad = jnp.zeros((LAYER_ROWS - LAYERS, 2 * LANES), jnp.float32)
+    step = 16 * LANES
+
+    def product_of(n, carry):
+        def columns_of(k):
+            return pl.ds(pl.multiple_of(n * step + 2 * k * LANES, 2 * LANES), 2 * LANES)
+
+        tiles = []
+        for k in range(8):
+            tiles += [cot[:, columns_of(k)], pad]
+        values = jnp.concatenate(tiles, axis=0)
+        values_high = values.astype(half)
+        values_low = (values - values_high.astype(jnp.float32)).astype(half)
+        result = dot(high, values_high) + (dot(high, values_low) + dot(low, values_high))
+        for k in range(8):
+            adj[:, columns_of(k)] = result[k * LAYER_ROWS : k * LAYER_ROWS + LAYERS]
+        return carry
+
+    lax.fori_loop(0, COLUMNS // step, product_of, 0)
+    adj_copy = pltpu.make_async_copy(adj, adj_hbm, out_sem.at[2])
+    adj_copy.start()
 
     chan_low.wait_recv()
     chan_high.wait_recv()
@@ -298,14 +345,11 @@
 
     pad0 = LEVELS[0][1]
 
-    def give_back(order, carry):
+    for order in range(TILES - 1):
         target = far_first(order)
         post(
             back_send.at[rows_at(target * MSG, RUN)], lev0.at[a, pl.ds(pad0, RUN)], 10, {"col": target}
         )
-        return carry
-
-    lax.fori_loop(0, TILES - 1, give_back, 0)
     own_back = pltpu.make_async_copy(
         back_send.at[rows_at(a * MSG, RUN)], lev0.at[a, pl.ds(pad0, RUN)], self_sem.at[2]
     )
@@ -413,76 +457,27 @@
         copy.wait_send()
     press_copy.wait()
     sens_copy.wait()
-
-
-def adjoint_kernel(
-    inverse_ref, cot_hbm, press_in, sens_in, grad_in,
-    adj_hbm, press_out, sens_out, grad_out,
-    cot, adj, press, sens, grad, in_sem, out_sem, pass_sem,
+    adj_copy.wait()
+
+
+def hand_on_kernel(
+    adj_in, press_in, sens_in, grad_in, adj_out, press_out, sens_out, grad_out, adj, press, sens, grad, in_sem, out_sem
 ):
-    pieces = in_sem.shape[0]
-    width = COLUMNS // pieces
-    outs, passes = [], []
-    for number, (src, dst) in enumerate(((press_in, press), (sens_in, sens), (grad_in, grad))):
-        copy = pltpu.make_async_copy(src, dst, pass_sem.at[number])
-        copy.start()
-        passes.append(copy)
-    ins = [
-        pltpu.make_async_copy(
-            cot_hbm.at[:, pl.ds(q * width, width)], cot.at[:, pl.ds(q * width, width)], in_sem.at[q]
-        )
-        for q in range(pieces)
-    ]
-    for copy in ins[:AHEAD]:
-        copy.start()
-    tall = 8 * LAYER_ROWS
-    half = jnp.bfloat16
-    dot = functools.partial(jnp.dot, preferred_element_type=jnp.float32)
-    layer = lax.rem(lax.broadcasted_iota(jnp.int32, (tall, LAYERS), 0), LAYER_ROWS)
-    spread = (layer == lax.broadcasted_iota(jnp.int32, (tall, LAYERS), 1)).astype(jnp.float32).astype(half)
-    block = lax.broadcasted_iota(jnp.int32, (tall, tall), 0) // LAYER_ROWS
-    own_block = block == lax.broadcasted_iota(jnp.int32, (tall, tall), 1) // LAYER_ROWS
-
-    def diagonal(part):
-        rows = dot(spread, part).astype(half)
-        full = lax.dot_general(rows, spread, (((1,), (1,)), ((), ())), preferred_element_type=jnp.float32)
-        return jnp.where(own_block, full, 0.0).astype(half)
-
-    matrix = inverse_ref[...].T
-    matrix_high = matrix.astype(half)
-    high = diagonal(matrix_high)
-    low = diagonal((matrix - matrix_high.astype(jnp.float32)).astype(half))
-    pad = jnp.zeros((LAYER_ROWS - LAYERS, 2 * LANES), jnp.float32)
-    step = 16 * LANES
-    for q in range(pieces):
-        ins[q].wait()
-        if q + AHEAD < pieces:
-            ins[q + AHEAD].start()
-        for start in range(q * width, (q + 1) * width, step):
-            tiles = []
-            for k in range(8):
-                tiles += [cot[:, start + 2 * k * LANES : start + 2 * (k + 1) * LANES], pad]
-            values = jnp.concatenate(tiles, axis=0)
-            values_high = values.astype(half)
-            values_low = (values - values_high.astype(jnp.float32)).astype(half)
-            result = dot(high, values_high) + (dot(high, values_low) + dot(low, values_high))
-            for k in range(8):
-                adj[:, start + 2 * k * LANES : start + 2 * (k + 1) * LANES] = result[
-                    k * LAYER_ROWS : k * LAYER_ROWS + LAYERS
-                ]
+    width = COLUMNS // PIECES
+    moves = [(press_in, press, press_out), (sens_in, sens, sens_out), (grad_in, grad, grad_out)]
+    for q in range(PIECES):
         at = pl.ds(q * width, width)
-        copy = pltpu.make_async_copy(adj.at[:, at], adj_hbm.at[:, at], out_sem.at[q])
-        copy.start()
-        outs.append(copy)
-        if q == 0:
-            for number, (src, dst) in enumerate(((press, press_out), (sens, sens_out), (grad, grad_out))):
-                passes[number].wait()
-                copy = pltpu.make_async_copy(src, dst, pass_sem.at[number])
-                copy.start()
-                outs.append(copy)
-    for copy in outs:
-        copy.wait()
-
+        moves.append((adj_in.at[:, at], adj.at[:, at], adj_out.at[:, at]))
+    ins, outs = [], []
+    for number, (src, held, dst) in enumerate(moves):
+        ins.append(pltpu.make_async_copy(src, held, in_sem.at[number]))
+        outs.append(pltpu.make_async_copy(held, dst, out_sem.at[number]))
+        ins[-1].start()
+    for came, goes in zip(ins, outs):
+        came.wait()
+        goes.start()
+    for goes in outs:
+        goes.wait()
 
 def on_device(
     velocity_cotangent,
@@ -508,17 +503,18 @@
     received = pltpu.VMEM(((TALL + 1) * MSG, LANES), f32)
     field = pltpu.VMEM((TALL, WIDE), f32)
     dma = pltpu.SemaphoreType.DMA
-    pressure, sensitivity, gradient = pl.pallas_call(
+    results = pl.pallas_call(
         kernel,
         out_shape=(
+            jax.ShapeDtypeStruct((LAYERS, COLUMNS), f32),
             jax.ShapeDtypeStruct((TILES, RUN * LANES), f32),
             jax.ShapeDtypeStruct((ROWS, LANES), f32),
             jax.ShapeDtypeStruct((1, CONTROLS), f32),
         ),
         in_specs=[pl.BlockSpec(memory_space=pltpu.SMEM), vmem] + [anywhere] * 9,
-        out_specs=(anywhere, anywhere, vmem),
+        out_specs=(anywhere, anywhere, anywhere, vmem),
         scratch_shapes=[
-            pltpu.VMEM((LAYERS, COLUMNS), f32),
+            pltpu.VMEM((LAYERS, COLUMNS), f32), pltpu.VMEM((LAYERS, COLUMNS), f32),
             pltpu.VMEM((CONTROLS, COLUMNS), jnp.bfloat16),
             columns, columns, numbers, padded, padded, numbers,
             pltpu.VMEM((TILES, RUN * LANES), jnp.int32),
@@ -530,30 +526,21 @@
         + [pltpu.VMEM((nodes, pad + tall, LANES), f32) for nodes, pad, tall in LEVELS]
         + [
             columns, pltpu.VMEM((CHIPS, ROWS, LANES), f32), columns, columns, columns,
-            dma((8,)), dma((PARTS,)), dma((3,)), dma((11,)), dma((11,)),
-            dma((PARTS, CHIPS - 1)), dma((PARTS, CHIPS - 1)), dma((PARTS,)), dma((PARTS,)), dma((2,)),
+            pltpu.SMEM((TILES + 1,), jnp.int32), dma((8,)), dma((PARTS,)), dma((3,)), dma((11,)), dma((11,)),
+            dma((PARTS, CHIPS - 1)), dma((PARTS, CHIPS - 1)), dma((PARTS,)), dma((PARTS,)), dma((3,)),
         ],
         compiler_params=pltpu.CompilerParams(
             collective_id=0, has_side_effects=True, vmem_limit_bytes=VMEM_BYTES
         ),
     )(group_mix, vertical_inverse, velocity_cotangent, *shaped, channel_open, control_map)
     adjoint, pressure, sensitivity, gradient = pl.pallas_call(
-        adjoint_kernel,
-        out_shape=(
-            jax.ShapeDtypeStruct((LAYERS, COLUMNS), f32),
-            jax.ShapeDtypeStruct((TILES, RUN * LANES), f32),
-            jax.ShapeDtypeStruct((ROWS, LANES), f32),
-            jax.ShapeDtypeStruct((1, CONTROLS), f32),
-        ),
-        in_specs=[vmem] + [anywhere] * 4,
+        hand_on_kernel,
+        out_shape=tuple(jax.ShapeDtypeStruct(x.shape, x.dtype) for x in results),
+        in_specs=[anywhere] * 4,
         out_specs=(anywhere,) * 4,
-        scratch_shapes=[
-            pltpu.VMEM((LAYERS, COLUMNS), f32), pltpu.VMEM((LAYERS, COLUMNS), f32),
-            pltpu.VMEM((TILES, RUN * LANES), f32), columns, pltpu.VMEM((1, CONTROLS), f32),
-            dma((PIECES,)), dma((PIECES,)), dma((3,)),
-        ],
+        scratch_shapes=[pltpu.VMEM(x.shape, x.dtype) for x in results] + [dma((3 + PIECES,)), dma((3 + PIECES,))],
         compiler_params=pltpu.CompilerParams(vmem_limit_bytes=VMEM_BYTES),
-    )(vertical_inverse, velocity_cotangent, pressure, sensitivity, gradient)
+    )(*results)
     return adjoint, pressure, sensitivity.reshape(COLUMNS), gradient.reshape(CONTROLS)
 
 

time: 54 us -> 52.4 us (0.970)
  Pallas kernels: 53.1 us -> 51.6 us
    pallas_call x2, Pallas kernels: 53.1 us -> 51.6 us  [the longest x1 48.5 us: on_device(): pl.pallas_call(kernel, out_shape=(jax.ShapeDtypeStruct((LAYERS, COLUMNS),...]
where the time goes in v4:
time: 52.4 us; the launch traced here: 52.3 us
  Pallas kernels  51.6 us (98%)
  between operations  0.64 us (1%)
    pallas_call x1, Pallas kernels, on_device(): pl.pallas_call(kernel, out_shape=(jax.ShapeDtypeStruct((LAYERS, COLUMNS),...  48.5 us
    pallas_call x1, Pallas kernels, on_device(): pl.pallas_call(hand_on_kernel, out_shape=tuple((jax.ShapeDtypeStruct(x.sh...  3.11 us

profile of v4, /device:TPU:1, one launch (start us, length us, event | category | flops | bytes accessed | tf_op | source)
XLA Modules:
  0.0 52.3 jit_solution(14791521159538480502)
XLA Ops:
  0.6 48.5 %shard_map.138 = (f32[20,32768]{1,0:T(8,128)}, f32[32,1280]{1,0:T(8,128)}, f32[256,128]{1,0:T(8,128)}, f32[1,64]{1,0:T(1,128)}) custom-call(f32[8,8]{1,0:T(8,128)} %mix_ref.1, f32[20,20]{1,0:T(8,128)} %inverse_ref.1, f32[20,32768]{1,0:T(8,128)} %cot_hbm.1, f32[256,128]{1,0:T(8,128)} %bitcast.8, f32[256,128]{1,0:T(8,128)} %bitcast.9, s32[256,128]{1,0:T(8,128)} %bitcast.10, ...), custom_call_target="tpu_custom_call" | custom-call | tf_op jit(solution)/shard_map/pallas_call | solution.py:506
  49.1 3.1 %shard_map.139 = (f32[20,32768]{1,0:T(8,128)}, f32[32,1280]{1,0:T(8,128)}, f32[256,128]{1,0:T(8,128)}, f32[1,64]{1,0:T(1,128)}) custom-call(f32[20,32768]{1,0:T(8,128)} %get-tuple-element.12.adj_in, f32[32,1280]{1,0:T(8,128)} %get-tuple-element.13.press_in, f32[256,128]{1,0:T(8,128)} %get-tuple-element.14.sens_in, f32[1,64]{1,0:T(1,128)} %get-tuple-element.15.grad_in), custom_call_target="tpu_custom_call" | custom-call | tf_op jit(solution)/shard_map/pallas_call | solution.py:536

commit v5 on v4

--- a/solution.py
+++ b/solution.py
@@ -29,6 +29,7 @@
 PIECES = 4
 PARTS = 4
 PART = ROWS // PARTS
+PART_ORDER = [q + half for q in range(PARTS // 2) for half in (0, PARTS // 2)]
 MESH = pl.DeviceIdType.MESH
 VMEM_BYTES = 64 * 1024 * 1024
 
@@ -43,7 +44,7 @@
     mix_ref, inverse_ref, cot_hbm, slide_hbm, fric_hbm, thaw_hbm, melt_hbm, store_hbm, owner_hbm, open_hbm, map_hbm,
     adj_hbm, press_hbm, sens_hbm, grad_ref,
     cot, adj, cmap, slide, fric, thaw, melt, store, owner, chan, source, basal,
-    send1, send2, recv1, recv2, cond, cond_low, cond_high, coef, pressure, press_out, back_send,
+    send1, send2, recv1, recv2, edge2, cond, cond_low, cond_high, coef, pressure, press_out, back_send,
     lev0, lev1, lev2, lev3, lev4, sens, gathered, other_send, other_recv, mine,
     begins, load_sem, cot_sem, self_sem, send_sem, recv_sem, part_send, part_recv, pair_send, pair_recv, out_sem,
 ):
@@ -96,9 +97,10 @@
 
     lane = lax.broadcasted_iota(jnp.int32, (1, LANES), 1)
     edge_rows = jnp.zeros((4 * MSG, LANES), jnp.float32)
-    for ref in (recv1, recv2):
-        ref[0 : 4 * MSG, :] = edge_rows
-        ref[(TALL - 4) * MSG : TALL * MSG, :] = edge_rows
+    recv1[0 : 4 * MSG, :] = edge_rows
+    recv1[(TALL - 4) * MSG : TALL * MSG, :] = edge_rows
+    edge2[0 : 4 * MSG, :] = edge_rows
+    edge2[(EDGE + 4) * MSG : 2 * EDGE * MSG, :] = edge_rows
 
     owner_load.wait()
     owners = owner[...]
@@ -276,19 +278,17 @@
     chan_up = post(cond.at[pl.ds(EDGE, EDGE)], cond.at[pl.ds(EDGE + TILES, EDGE)], 4, {"grp": up})
     chan_down = post(cond.at[pl.ds(TILES, EDGE)], cond.at[pl.ds(0, EDGE)], 5, {"grp": down})
 
-    def rows_beside(buffer, number):
-        first = post(
-            buffer.at[pl.ds(EDGE * MSG, 4 * MSG)], buffer.at[pl.ds((EDGE + TILES) * MSG, 4 * MSG)], number, {"grp": up}
-        )
+    def rows_beside(buffer, into, below, number):
+        first = post(buffer.at[pl.ds(EDGE * MSG, 4 * MSG)], into.at[pl.ds(below, 4 * MSG)], number, {"grp": up})
         second = post(
-            buffer.at[pl.ds((TILES + 4) * MSG, 4 * MSG)], buffer.at[pl.ds(4 * MSG, 4 * MSG)], number + 1, {"grp": down}
+            buffer.at[pl.ds((TILES + 4) * MSG, 4 * MSG)], into.at[pl.ds(4 * MSG, 4 * MSG)], number + 1, {"grp": down}
         )
         return first, second
 
     others = (TILES - 1) * MSG
     own1.wait()
     all_done(recv1, others, recv_sem.at[2])
-    rows1 = rows_beside(recv1, 6)
+    rows1 = rows_beside(recv1, recv1, (EDGE + TILES) * MSG, 6)
     chan_up.wait_recv()
     chan_down.wait_recv()
     for copy in rows1:
@@ -308,79 +308,101 @@
 
     own2.wait()
     all_done(recv2, others, recv_sem.at[3])
-    rows2 = rows_beside(recv2, 8)
+    rows2 = rows_beside(recv2, edge2, EDGE * MSG, 8)
+
+    last = slice(RUN * LANES, WIDE)
+    lane_tall = lax.broadcasted_iota(jnp.int32, (TILES, LANES), 1)
+    used = jnp.logical_or(lane_tall < 4, lane_tall >= LANES - 4)
+
+    def sweeps(got1, got2, inside, rate_of):
+        side = got2(15)
+        store_side = jnp.where(lane_tall < 64, pltpu.roll(side, LANES - 4, 1), pltpu.roll(side, 4, 1))
+        store_side = jnp.where(used, store_side, 0.0)
+        melts = [got1(RUN + k) for k in range(MSG - RUN)]
+        melts += [got2(k) for k in range(2 * RUN - MSG)] + [jnp.where(used, side, 0.0)]
+        keep = jnp.concatenate([1.0 - melt_rate * part for part in melts], axis=1)
+        rate_side = jnp.where(inside, rate_of(cond, last) / (1.0 + store_side), 0.0)
+        rate = jnp.concatenate([rate_of(coef, slice(0, RUN * LANES)), rate_side], axis=1)
+        pressure[...] = jnp.concatenate(
+            [jnp.where(inside, got2(2 * RUN - MSG + k), 0.0) for k in range(RUN + 1)], axis=1
+        )
+        for sweep in range(HSWEEPS):
+            field = pressure[...]
+            sides = (
+                pltpu.roll(field, 1, 1)
+                + pltpu.roll(field, WIDE - 1, 1)
+                + pltpu.roll(field, 1, 0)
+                + pltpu.roll(field, TILES - 1, 0)
+            )
+            pressure[...] = keep * field + rate * (sides - 4.0 * field)
+
+    def own_rows(ref):
+        return lambda k: ref[pl.ds(EDGE * MSG + k, TILES, stride=MSG), :]
+
+    pad0 = LEVELS[0][1]
+
+    def give_back(interior):
+        def one(order, carry):
+            target = far_first(order)
+            middle = jnp.logical_and(target >= 4, target < TILES - 4)
+
+            @pl.when(middle if interior else jnp.logical_not(middle))
+            def _():
+                post(
+                    back_send.at[rows_at(target * MSG, RUN)], lev0.at[a, pl.ds(pad0, RUN)], 10, {"col": target}
+                )
+
+            return carry
+
+        lax.fori_loop(0, TILES - 1, one, 0)
+
+    sweeps(own_rows(recv1), own_rows(recv2), True, lambda ref, at: ref[EDGE : EDGE + TILES, at])
+    for k in range(RUN):
+        at = slice(k * LANES, (k + 1) * LANES)
+        for i in range(TILES // 8):
+            back_send[pl.ds(8 * i * MSG + k, 8, stride=MSG), :] = pressure[8 * i : 8 * i + 8, at]
+    press_out[...] = pressure[:, : RUN * LANES]
+    give_back(True)
+
     for copy in rows2:
         copy.wait_recv()
 
-    side = mesh_rows(recv2, 15)
-    lane_tall = lax.broadcasted_iota(jnp.int32, (TALL, LANES), 1)
-    store_side = jnp.where(lane_tall < 64, pltpu.roll(side, LANES - 4, 1), pltpu.roll(side, 4, 1))
-    used = jnp.logical_or(lane_tall < 4, lane_tall >= LANES - 4)
-    store_side = jnp.where(used, store_side, 0.0)
-    melt_side = jnp.where(used, side, 0.0)
-    at = slice(RUN * LANES, WIDE)
-    coef[:, at] = jnp.where(inside, cond[:, at] / (1.0 + store_side), 0.0)
-    melts = [mesh_rows(recv1, RUN + k) for k in range(MSG - RUN)]
-    melts += [mesh_rows(recv2, k) for k in range(2 * RUN - MSG)] + [melt_side]
-    keeps = [1.0 - melt_rate * part for part in melts]
-    now = [jnp.where(inside, mesh_rows(recv2, 2 * RUN - MSG + k), 0.0) for k in range(RUN + 1)]
-    keep = jnp.concatenate(keeps, axis=1)
-    field = jnp.concatenate(now, axis=1)
-    pressure[...] = field
-    for sweep in range(HSWEEPS):
-        field = pressure[...]
-        rate = coef[...]
-        sides = (
-            pltpu.roll(field, 1, 1) + pltpu.roll(field, WIDE - 1, 1) + pltpu.roll(field, 1, 0) + pltpu.roll(field, TALL - 1, 0)
-        )
-        pressure[...] = keep * field + rate * (sides - 4.0 * field)
-
+    def band(ref, k):
+        return [ref[pl.ds(row * MSG + k, EDGE, stride=MSG), :] for row in (EDGE, TILES)]
+
+    def edge_rows1(k):
+        outer = [recv1[pl.ds(row * MSG + k, EDGE, stride=MSG), :] for row in (0, EDGE + TILES)]
+        inner = band(recv1, k)
+        return jnp.concatenate([outer[0], inner[0], inner[1], outer[1]], axis=0)
+
+    def edge_rows2(k):
+        outer = [edge2[pl.ds(row * MSG + k, EDGE, stride=MSG), :] for row in (0, EDGE)]
+        inner = band(recv2, k)
+        return jnp.concatenate([outer[0], inner[0], inner[1], outer[1]], axis=0)
+
+    band_row = lax.broadcasted_iota(jnp.int32, (TILES, LANES), 0)
+    band_inside = jnp.logical_and(
+        jnp.logical_or(band_row >= EDGE, g > 0), jnp.logical_or(band_row < TILES - EDGE, g < GROUP - 1)
+    )
+    sweeps(
+        edge_rows1, edge_rows2, band_inside,
+        lambda ref, at: jnp.concatenate([ref[0 : 2 * EDGE, at], ref[TILES:TALL, at]], axis=0),
+    )
     for k in range(RUN):
-        for i in range(TILES // 8):
-            cells = pressure[EDGE + 8 * i : EDGE + 8 * i + 8, k * LANES : (k + 1) * LANES]
-            back_send[pl.ds(8 * i * MSG + k, 8, stride=MSG), :] = cells
-    press_out[...] = pressure[EDGE : EDGE + TILES, : RUN * LANES]
+        at = slice(k * LANES, (k + 1) * LANES)
+        back_send[pl.ds(k, 4, stride=MSG), :] = pressure[EDGE : EDGE + 4, at]
+        back_send[pl.ds((TILES - 4) * MSG + k, 4, stride=MSG), :] = pressure[2 * EDGE + 4 : 3 * EDGE, at]
+    give_back(False)
+    press_out[0:4, :] = pressure[EDGE : EDGE + 4, : RUN * LANES]
+    press_out[TILES - 4 : TILES, :] = pressure[2 * EDGE + 4 : 3 * EDGE, : RUN * LANES]
     press_copy = pltpu.make_async_copy(press_out, press_hbm, out_sem.at[0])
     press_copy.start()
-
-    pad0 = LEVELS[0][1]
-
-    for order in range(TILES - 1):
-        target = far_first(order)
-        post(
-            back_send.at[rows_at(target * MSG, RUN)], lev0.at[a, pl.ds(pad0, RUN)], 10, {"col": target}
-        )
     own_back = pltpu.make_async_copy(
         back_send.at[rows_at(a * MSG, RUN)], lev0.at[a, pl.ds(pad0, RUN)], self_sem.at[2]
     )
     own_back.start()
     own_back.wait()
     all_done(back_send, (TILES - 1) * RUN, recv_sem.at[10])
-
-    levels = (lev0, lev1, lev2, lev3, lev4)
-    for level, (nodes, pad, tall) in enumerate(LEVELS):
-        ref = levels[level]
-        index = lax.broadcasted_iota(jnp.int32, (tall, LANES), 0) * LANES + lax.broadcasted_iota(
-            jnp.int32, (tall, LANES), 1
-        )
-        for node in range(nodes // 2):
-            begin = starts[(2 * node) << level]
-            length = jnp.clip(starts[(2 * node + 1) << level] - begin, 0, (RUN << level) * LANES)
-            first = lax.shift_right_logical(length, 7)
-            turn = lax.bitwise_and(length, LANES - 1)
-            mine_rows = ref[2 * node, pl.ds(pad, tall), :]
-            here = pltpu.roll(ref[2 * node + 1, pl.ds(pad - first, tall), :], turn, 1)
-            before = pltpu.roll(ref[2 * node + 1, pl.ds(pad - 1 - first, tall), :], turn, 1)
-            moved = jnp.where(lane >= turn, here, before)
-            merged = jnp.where(index < length, mine_rows, moved)
-            if level < len(LEVELS) - 1:
-                levels[level + 1][node, pl.ds(LEVELS[level + 1][1], tall), :] = merged
-            else:
-                value = thaw[...].astype(jnp.float32) * fric[...] * (basal[...] + merged)
-                sens[...] = value
-
-    sens_copy = pltpu.make_async_copy(sens, sens_hbm, out_sem.at[1])
-    sens_copy.start()
 
     def pass_on(q, slot, src, ahead):
         copy = pltpu.make_async_remote_copy(
@@ -395,10 +417,43 @@
         return copy
 
     parts = {}
-    for q in range(PARTS):
-        parts[q, 1] = pass_on(q, 1, sens, 1)
-        other = (q + PARTS // 2) % PARTS
-        parts[other, 3] = pass_on(other, 3, sens, CHIPS - 1)
+
+    def merge(ref, node, pad, length, begin, rows):
+        first = lax.shift_right_logical(length, 7)
+        turn = lax.bitwise_and(length, LANES - 1)
+        index = lax.broadcasted_iota(jnp.int32, (rows, LANES), 0) * LANES + lax.broadcasted_iota(
+            jnp.int32, (rows, LANES), 1
+        )
+        head = ref[2 * node, pl.ds(pad + begin, rows), :]
+        here = pltpu.roll(ref[2 * node + 1, pl.ds(pad + begin - first, rows), :], turn, 1)
+        before = pltpu.roll(ref[2 * node + 1, pl.ds(pad + begin - 1 - first, rows), :], turn, 1)
+        return jnp.where(index < length - begin * LANES, head, jnp.where(lane >= turn, here, before))
+
+    levels = (lev0, lev1, lev2, lev3, lev4)
+    for level, (nodes, pad, tall) in enumerate(LEVELS):
+        ref = levels[level]
+        for node in range(nodes // 2):
+            begin = starts[(2 * node) << level]
+            length = jnp.clip(starts[(2 * node + 1) << level] - begin, 0, (RUN << level) * LANES)
+            for part, rows in ((0, tall),) if level < len(LEVELS) - 1 else tuple((q, PART) for q in PART_ORDER):
+                merged = merge(ref, node, pad, length, part * rows, rows)
+                if level < len(LEVELS) - 1:
+                    levels[level + 1][node, pl.ds(LEVELS[level + 1][1], tall), :] = merged
+                else:
+                    at = pl.ds(part * PART, PART)
+                    sens[at, :] = thaw[at, :].astype(jnp.float32) * fric[at, :] * (basal[at, :] + merged)
+                    if part < PARTS // 2:
+                        parts[part, 1] = pass_on(part, 1, sens, 1)
+                    else:
+                        parts[part, 3] = pass_on(part, 3, sens, CHIPS - 1)
+
+    sens_copy = pltpu.make_async_copy(sens, sens_hbm, out_sem.at[1])
+    sens_copy.start()
+
+    for q in range(PARTS // 2):
+        other = q + PARTS // 2
+        parts[other, 1] = pass_on(other, 1, sens, 1)
+        parts[q, 3] = pass_on(q, 3, sens, CHIPS - 1)
     in_order = []
     for q in range(PARTS // 2):
         other = q + PARTS // 2
@@ -519,9 +574,9 @@
             columns, columns, numbers, padded, padded, numbers,
             pltpu.VMEM((TILES, RUN * LANES), jnp.int32),
             padded, columns,
-            messages, messages, received, received,
+            messages, messages, received, received, pltpu.VMEM(((2 * EDGE + 1) * MSG, LANES), f32),
             field, pltpu.VMEM((TILES, LANES), f32), pltpu.VMEM((TILES, LANES), f32),
-            field, field, pltpu.VMEM((TILES, RUN * LANES), f32), messages,
+            field, pltpu.VMEM((TILES, WIDE), f32), pltpu.VMEM((TILES, RUN * LANES), f32), messages,
         ]
         + [pltpu.VMEM((nodes, pad + tall, LANES), f32) for nodes, pad, tall in LEVELS]
         + [

time: 52.4 us -> 51 us (0.973)
  Pallas kernels: 51.6 us -> 50.2 us
    pallas_call x1, Pallas kernels: 48.5 us -> 47.1 us  [on_device(): pl.pallas_call(kernel, out_shape=(jax.ShapeDtypeStruct((LAYERS, COLUMNS),...]
where the time goes in v5:
time: 51 us; the launch traced here: 50.9 us
  Pallas kernels  50.2 us (98%)
  between operations  0.64 us (1%)
    pallas_call x1, Pallas kernels, on_device(): pl.pallas_call(kernel, out_shape=(jax.ShapeDtypeStruct((LAYERS, COLUMNS),...  47.1 us
    pallas_call x1, Pallas kernels, on_device(): pl.pallas_call(hand_on_kernel, out_shape=tuple((jax.ShapeDtypeStruct(x.sh...  3.11 us

profile of v5, /device:TPU:1, one launch (start us, length us, event | category | flops | bytes accessed | tf_op | source)
XLA Modules:
  0.0 50.9 jit_solution(4423547874374125742)
XLA Ops:
  0.6 47.1 %shard_map.138 = (f32[20,32768]{1,0:T(8,128)}, f32[32,1280]{1,0:T(8,128)}, f32[256,128]{1,0:T(8,128)}, f32[1,64]{1,0:T(1,128)}) custom-call(f32[8,8]{1,0:T(8,128)} %mix_ref.1, f32[20,20]{1,0:T(8,128)} %inverse_ref.1, f32[20,32768]{1,0:T(8,128)} %cot_hbm.1, f32[256,128]{1,0:T(8,128)} %bitcast.8, f32[256,128]{1,0:T(8,128)} %bitcast.9, s32[256,128]{1,0:T(8,128)} %bitcast.10, ...), custom_call_target="tpu_custom_call" | custom-call | tf_op jit(solution)/shard_map/pallas_call | solution.py:561
  47.8 3.1 %shard_map.139 = (f32[20,32768]{1,0:T(8,128)}, f32[32,1280]{1,0:T(8,128)}, f32[256,128]{1,0:T(8,128)}, f32[1,64]{1,0:T(1,128)}) custom-call(f32[20,32768]{1,0:T(8,128)} %get-tuple-element.12.adj_in, f32[32,1280]{1,0:T(8,128)} %get-tuple-element.13.press_in, f32[256,128]{1,0:T(8,128)} %get-tuple-element.14.sens_in, f32[1,64]{1,0:T(1,128)} %get-tuple-element.15.grad_in), custom_call_target="tpu_custom_call" | custom-call | tf_op jit(solution)/shard_map/pallas_call | solution.py:591

commit v6 on v5

--- a/solution.py
+++ b/solution.py
@@ -22,6 +22,7 @@
 ROWS = COLUMNS // LANES
 RUN = 10
 MSG = 16
+MSG2 = 15
 EDGE = 8
 WIDE = RUN * LANES + LANES
 TALL = TILES + 2 * EDGE
@@ -134,9 +135,9 @@
         copy.start()
         return copy
 
-    def keep_own(src, dst, self_number):
+    def keep_own(src, dst, self_number, rows):
         own = pltpu.make_async_copy(
-            src.at[rows_at(a * MSG, MSG)], dst.at[rows_at((EDGE + a) * MSG, MSG)], self_sem.at[self_number]
+            src.at[rows_at(a * MSG, rows)], dst.at[rows_at((EDGE + a) * MSG, rows)], self_sem.at[self_number]
         )
         own.start()
         return own
@@ -149,14 +150,14 @@
         away_y = outward(RING_Y // 2, order % RING_Y)
         return lax.rem(a // RING_Z + away_y, RING_Y) * RING_Z + lax.rem(a + away_z, RING_Z)
 
-    def to_all(src, dst, number, self_number):
+    def to_all(src, dst, number, self_number, rows):
         def one(order, carry):
             target = far_first(order)
-            post(src.at[rows_at(target * MSG, MSG)], dst.at[rows_at((EDGE + a) * MSG, MSG)], number, {"col": target})
+            post(src.at[rows_at(target * MSG, rows)], dst.at[rows_at((EDGE + a) * MSG, rows)], number, {"col": target})
             return carry
 
         lax.fori_loop(0, TILES - 1, one, 0)
-        return keep_own(src, dst, self_number)
+        return keep_own(src, dst, self_number, rows)
 
     def all_done(buffer, rows, sem):
         pltpu.make_async_copy(buffer.at[pl.ds(0, rows)], buffer.at[pl.ds(0, rows)], sem).wait()
@@ -177,7 +178,7 @@
             pl.semaphore_wait(barrier, TILES - 1 + 2 + 2)
         for t in targets[: TILES - 1 - group * 8]:
             post(send1.at[rows_at(t * MSG, MSG)], recv1.at[rows_at((EDGE + a) * MSG, MSG)], 2, {"col": t})
-    own1 = keep_own(send1, recv1, 0)
+    own1 = keep_own(send1, recv1, 0, MSG)
     chan_load.wait()
     cond[EDGE : EDGE + TILES, : RUN * LANES] = jnp.where(chan[...] == 1, diffusion_rate, 0.25 * diffusion_rate)
     chan_low = post(cond.at[EDGE : EDGE + TILES, (RUN - 1) * LANES : RUN * LANES], cond_low, 0, {"col": right})
@@ -219,16 +220,20 @@
     def every(ref, row):
         return ref[pl.ds(row, TILES, stride=MSG), :]
 
-    send2[pl.ds(14, TILES, stride=MSG), :] = beside(every(send2, 4), every(send2, 13))
+    source_sides = beside(every(send2, 4), every(send2, 13))
     melt_sides = beside(every(send1, 10), every(send2, 3))
     store_sides = beside(every(send1, 0), every(send1, 9))
-    store_moved = jnp.where(
-        lanes < 64, pltpu.roll(store_sides, 4, 1), pltpu.roll(store_sides, LANES - 4, 1)
-    )
-    send2[pl.ds(15, TILES, stride=MSG), :] = jnp.where(
-        jnp.logical_or(lanes < 4, lanes >= LANES - 4), melt_sides, store_moved
-    )
-    own2 = to_all(send2, recv2, 3, 1)
+
+    def moved_in(sides, by):
+        return jnp.where(lanes < 64, pltpu.roll(sides, by, 1), pltpu.roll(sides, LANES - by, 1))
+
+    def outer(count):
+        return jnp.logical_or(lanes < count, lanes >= LANES - count)
+
+    send2[pl.ds(14, TILES, stride=MSG), :] = jnp.where(
+        outer(4), source_sides, jnp.where(outer(8), moved_in(melt_sides, 4), moved_in(store_sides, 8))
+    )
+    own2 = to_all(send2, recv2, 3, 1, MSG2)
 
     tall = 8 * LAYER_ROWS
     half = jnp.bfloat16
@@ -307,7 +312,7 @@
         coef[:, at] = jnp.where(inside, cond[:, at] / (1.0 + mesh_rows(recv1, k)), 0.0)
 
     own2.wait()
-    all_done(recv2, others, recv_sem.at[3])
+    all_done(recv2, (TILES - 1) * MSG2, recv_sem.at[3])
     rows2 = rows_beside(recv2, edge2, EDGE * MSG, 8)
 
     last = slice(RUN * LANES, WIDE)
@@ -315,16 +320,22 @@
     used = jnp.logical_or(lane_tall < 4, lane_tall >= LANES - 4)
 
     def sweeps(got1, got2, inside, rate_of):
-        side = got2(15)
-        store_side = jnp.where(lane_tall < 64, pltpu.roll(side, LANES - 4, 1), pltpu.roll(side, 4, 1))
-        store_side = jnp.where(used, store_side, 0.0)
+        side = got2(14)
+
+        def moved_out(by):
+            back = jnp.where(lane_tall < 64, pltpu.roll(side, LANES - by, 1), pltpu.roll(side, by, 1))
+            return jnp.where(used, back, 0.0)
+
+        store_side = moved_out(8)
         melts = [got1(RUN + k) for k in range(MSG - RUN)]
-        melts += [got2(k) for k in range(2 * RUN - MSG)] + [jnp.where(used, side, 0.0)]
+        melts += [got2(k) for k in range(2 * RUN - MSG)] + [moved_out(4)]
         keep = jnp.concatenate([1.0 - melt_rate * part for part in melts], axis=1)
         rate_side = jnp.where(inside, rate_of(cond, last) / (1.0 + store_side), 0.0)
         rate = jnp.concatenate([rate_of(coef, slice(0, RUN * LANES)), rate_side], axis=1)
         pressure[...] = jnp.concatenate(
-            [jnp.where(inside, got2(2 * RUN - MSG + k), 0.0) for k in range(RUN + 1)], axis=1
+            [jnp.where(inside, got2(2 * RUN - MSG + k), 0.0) for k in range(RUN)]
+            + [jnp.where(jnp.logical_and(inside, used), side, 0.0)],
+            axis=1,
         )
         for sweep in range(HSWEEPS):
             field = pressure[...]
@@ -341,20 +352,27 @@
 
     pad0 = LEVELS[0][1]
 
-    def give_back(interior):
-        def one(order, carry):
-            target = far_first(order)
-            middle = jnp.logical_and(target >= 4, target < TILES - 4)
-
-            @pl.when(middle if interior else jnp.logical_not(middle))
-            def _():
-                post(
-                    back_send.at[rows_at(target * MSG, RUN)], lev0.at[a, pl.ds(pad0, RUN)], 10, {"col": target}
-                )
-
-            return carry
-
-        lax.fori_loop(0, TILES - 1, one, 0)
+    def give_back(target):
+        post(back_send.at[rows_at(target * MSG, RUN)], lev0.at[a, pl.ds(pad0, RUN)], 10, {"col": target})
+
+    def middle_back(order, carry):
+        target = far_first(order)
+
+        @pl.when(jnp.logical_and(target >= 4, target < TILES - 4))
+        def _():
+            give_back(target)
+
+        return carry
+
+    def edge_back(order, carry):
+        number = lax.rem(a + order, 8)
+        target = number + (number // 4) * (TILES - 8)
+
+        @pl.when(target != a)
+        def _():
+            give_back(target)
+
+        return carry
 
     sweeps(own_rows(recv1), own_rows(recv2), True, lambda ref, at: ref[EDGE : EDGE + TILES, at])
     for k in range(RUN):
@@ -362,7 +380,7 @@
         for i in range(TILES // 8):
             back_send[pl.ds(8 * i * MSG + k, 8, stride=MSG), :] = pressure[8 * i : 8 * i + 8, at]
     press_out[...] = pressure[:, : RUN * LANES]
-    give_back(True)
+    lax.fori_loop(0, TILES - 1, middle_back, 0)
 
     for copy in rows2:
         copy.wait_recv()
@@ -392,7 +410,7 @@
         at = slice(k * LANES, (k + 1) * LANES)
         back_send[pl.ds(k, 4, stride=MSG), :] = pressure[EDGE : EDGE + 4, at]
         back_send[pl.ds((TILES - 4) * MSG + k, 4, stride=MSG), :] = pressure[2 * EDGE + 4 : 3 * EDGE, at]
-    give_back(False)
+    lax.fori_loop(0, 8, edge_back, 0)
     press_out[0:4, :] = pressure[EDGE : EDGE + 4, : RUN * LANES]
     press_out[TILES - 4 : TILES, :] = pressure[2 * EDGE + 4 : 3 * EDGE, : RUN * LANES]
     press_copy = pltpu.make_async_copy(press_out, press_hbm, out_sem.at[0])
@@ -506,7 +524,7 @@
     for copy in rows1 + rows2:
         copy.wait_send()
     all_done(send1, others, send_sem.at[2])
-    all_done(send2, others, send_sem.at[3])
+    all_done(send2, (TILES - 1) * MSG2, send_sem.at[3])
     all_done(back_send, (TILES - 1) * RUN, send_sem.at[10])
     for copy in list(parts.values()) + list(pairs.values()):
         copy.wait_send()

time: 51 us -> 50.9 us (level)
  no operation moved by 1% of the time
where the time goes in v6:
time: 50.9 us; the launch traced here: 50.7 us
  Pallas kernels  50 us (98%)
  between operations  0.64 us (1%)
    pallas_call x1, Pallas kernels, on_device(): pl.pallas_call(kernel, out_shape=(jax.ShapeDtypeStruct((LAYERS, COLUMNS),...  46.9 us
    pallas_call x1, Pallas kernels, on_device(): pl.pallas_call(hand_on_kernel, out_shape=tuple((jax.ShapeDtypeStruct(x.sh...  3.11 us

profile of v6, /device:TPU:1, one launch (start us, length us, event | category | flops | bytes accessed | tf_op | source)
XLA Modules:
  0.0 50.7 jit_solution(2808719802461642704)
XLA Ops:
  0.6 46.9 %shard_map.138 = (f32[20,32768]{1,0:T(8,128)}, f32[32,1280]{1,0:T(8,128)}, f32[256,128]{1,0:T(8,128)}, f32[1,64]{1,0:T(1,128)}) custom-call(f32[8,8]{1,0:T(8,128)} %mix_ref.1, f32[20,20]{1,0:T(8,128)} %inverse_ref.1, f32[20,32768]{1,0:T(8,128)} %cot_hbm.1, f32[256,128]{1,0:T(8,128)} %bitcast.8, f32[256,128]{1,0:T(8,128)} %bitcast.9, s32[256,128]{1,0:T(8,128)} %bitcast.10, ...), custom_call_target="tpu_custom_call" | custom-call | tf_op jit(solution)/shard_map/pallas_call | solution.py:579
  47.6 3.1 %shard_map.139 = (f32[20,32768]{1,0:T(8,128)}, f32[32,1280]{1,0:T(8,128)}, f32[256,128]{1,0:T(8,128)}, f32[1,64]{1,0:T(1,128)}) custom-call(f32[20,32768]{1,0:T(8,128)} %get-tuple-element.12.adj_in, f32[32,1280]{1,0:T(8,128)} %get-tuple-element.13.press_in, f32[256,128]{1,0:T(8,128)} %get-tuple-element.14.sens_in, f32[1,64]{1,0:T(1,128)} %get-tuple-element.15.grad_in), custom_call_target="tpu_custom_call" | custom-call | tf_op jit(solution)/shard_map/pallas_call | solution.py:609
